TPU v7x, 32 devices: a whole 2x2x4 slice. The times are simulated.
32 devices in a mesh: slab: 4 (over x, core), modes: 8 (over z, y).
Axes of the slice: x: 2, y: 2, z: 4, core: 2. Of those that a mesh axis runs over, the one named last changes fastest.
Arguments:
- occupation_prior: float32 [512, 4096], P('slab', 'modes'), may hold values from -6 to 6
- coupling: bfloat16 [32, 8, 128, 128], P('modes'), may hold values from -0.25 to 0.25
- pattern: int32 [32, 8], P('modes'), may hold values from 0 to 3
- pseudo_weights: float32 [4096], P('modes'), may hold values from -0.09375 to 0.09375
- equilibrium_slope: float32 [4096], replicated, may hold values from 0.3 to 3
- direction: int32 [32], P('modes'), may hold values from 0 to 1
- stream_rate: float32 [4096], P('modes'), may hold values from 0.15 to 0.95
- inscatter: float32 [32, 128, 128], P('modes'), may hold values from -0.125 to 0.125
- inflow_low: float32 [4, 4096], P(None, 'modes'), may hold values from -6 to 6
- inflow_high: float32 [4, 4096], P(None, 'modes'), may hold values from -6 to 6
- front_of_row: int32 [16], replicated, may hold values from 0 to 3
Outputs:
- swept: float32 [512, 4096], P('slab', 'modes')
Inputs may be any that keep to these rules, and one draw needn't show every extreme that they name: `pattern`: each entry names one of the 4 blocks of a group.
All inputs are finite; a program needn't handle non-finite values.
Results may differ from a plain program's by a relative error of at most 0.002.
Values sent between devices are 32-bit elements; how exact they have to be, the bound alone decides.
A program may use at most 128 MiB of HBM per device.

v0:
```python
import jax
import jax.numpy as jnp
from jax import lax
from jax.sharding import PartitionSpec as P

BLK = 128
SHELL = 4


def shifted(block, axis, distance):
    devices = range(lax.axis_size(axis))
    route = [(i - distance, i) for i in devices if i - distance in devices]
    return lax.ppermute(block, axis, route)


def advance(face_now, power_matrix, shift_amount):
    return (
        jnp.einsum("ybk,bkl->ybl", face_now, power_matrix, precision=lax.Precision.HIGHEST)
        + shift_amount
    )


def summed_up(pieces):
    return jnp.sum(pieces, axis=1)


def per_device(
    occupation_prior,
    coupling,
    pattern,
    pseudo_weights,
    equilibrium_slope,
    direction,
    stream_rate,
    inscatter,
    inflow_low,
    inflow_high,
    front_of_row,
):
    cell_count, local_width = occupation_prior.shape
    group_count = coupling.shape[1]
    lateral = front_of_row.shape[0]
    rounded = occupation_prior.astype(jnp.bfloat16).reshape(cell_count, SHELL, BLK)
    products = jnp.einsum("cbk,bgkl->bcgl", rounded, coupling, preferred_element_type=jnp.float32)
    selected = pattern[:, :, None] == jnp.arange(SHELL, dtype=jnp.int32)[None, None, :]
    partial_term = jnp.sum(
        jnp.where(selected[:, None, :, :, None], products[:, :, :, None, :], 0.0), axis=0
    )
    partial_term = partial_term.reshape(cell_count, group_count * local_width)
    branch_pseudo_warmth = jnp.sum(occupation_prior * pseudo_weights[None, :], axis=1)
    sectioned = partial_term.reshape(cell_count, group_count, local_width)
    collided_branches = summed_up(
        lax.all_to_all(sectioned, "modes", split_axis=1, concat_axis=1, tiled=True)
    )
    local_specific_warmth = lax.dynamic_slice_in_dim(
        equilibrium_slope, lax.axis_index("modes") * local_width, local_width
    )
    pseudo_warmth_sum = lax.psum(branch_pseudo_warmth, "modes")
    gain_contribution = (
        collided_branches + pseudo_warmth_sum[:, None] * local_specific_warmth[None, :]
    )
    slab_cells = cell_count // lateral
    source_cells = gain_contribution.reshape(slab_cells, lateral, SHELL, BLK)
    forward_mask = (direction == 1)[None, None, :, None]
    ordered = jnp.where(forward_mask, source_cells, source_cells[::-1])
    rate_table = stream_rate.reshape(SHELL, BLK)
    transfer = jnp.eye(BLK, dtype=jnp.float32)[None] + inscatter
    step_matrix = rate_table[:, :, None] * transfer

    def local_sweep(carry, layer_source):
        previous, power_matrix = carry
        previous = jnp.einsum(
            "ybk,bkl->ybl",
            layer_source + rate_table * previous,
            transfer,
            precision=lax.Precision.HIGHEST,
        )
        following = jnp.einsum(
            "bkl,blm->bkm", power_matrix, step_matrix, precision=lax.Precision.HIGHEST
        )
        return ((previous, following), (previous, power_matrix))

    start_carry = (jnp.zeros((lateral, SHELL, BLK), jnp.float32), step_matrix)
    _, (particular, powers) = lax.scan(local_sweep, start_carry, ordered)
    row_picks = (
        front_of_row[:, None] == jnp.arange(inflow_low.shape[0], dtype=jnp.int32)[None, :]
    ).astype(jnp.float32)
    wall_low = jnp.dot(row_picks, inflow_low, precision=lax.Precision.HIGHEST).reshape(
        lateral, SHELL, BLK
    )
    wall_high = jnp.dot(row_picks, inflow_high, precision=lax.Precision.HIGHEST).reshape(
        lateral, SHELL, BLK
    )
    last_power = powers[-1]
    last_part = particular[-1]
    index_of_slab = lax.axis_index("slab")
    slab_count = lax.axis_size("slab")
    at_first = index_of_slab == 0
    at_final = index_of_slab == slab_count - 1

    def relay(turn_index, face_pair):
        low_face, high_face = face_pair
        moved_up = shifted(advance(low_face, last_power, last_part), "slab", 1)
        moved_down = shifted(advance(high_face, last_power, last_part), "slab", -1)
        return (jnp.where(at_first, wall_low, moved_up), jnp.where(at_final, wall_high, moved_down))

    from_low, from_high = lax.fori_loop(0, slab_count - 1, relay, (wall_low, wall_high))
    inflow = jnp.where(forward_mask[0], from_low, from_high)
    layers = particular + jnp.einsum(
        "ybk,xbkl->xybl", inflow, powers, precision=lax.Precision.HIGHEST
    )
    result = jnp.where(forward_mask, layers, layers[::-1])
    return result.reshape(cell_count, local_width)


def solution(mesh):
    placed = (
        P("slab", "modes"),
        P("modes", None, None, None),
        P("modes", None),
        P("modes"),
        P(),
        P("modes"),
        P("modes"),
        P("modes", None, None),
        P(None, "modes"),
        P(None, "modes"),
        P(),
    )
    return jax.shard_map(
        per_device, mesh=mesh, in_specs=placed, out_specs=P("slab", "modes"), check_vma=False
    )
```

profile of v0, /device:TPU:9, one launch (start us, length us, event | category | flops | bytes accessed | tf_op | source)
XLA Modules:
  0.0 114.0 jit_solution(3543239775985205319)
XLA Ops:
  0.0 1.2 %multiply_reduce_fusion = (f32[128]{0:T(128)S(1)}, bf16[128,512]{1,0:T(8,128)(2,1)S(1)}) fusion(f32[128,512]{1,0:T(8,128)} %param.15, f32[512]{0:T(512)} %param.18), kind=kLoop, calls=%fused_computation.26 | loop fusion | flops 196480 | bytes 395776 | tf_op jit(solution)/shard_map/reduce_sum | solution.py:50
  1.4 0.4 fusion.15
  1.8 1.2 %copy.55 = f32[4,128,8,128]{3,2,1,0:T(8,128)S(1)} copy(f32[4,128,8,128]{3,1,2,0:T(8,128)S(1)} %fusion.15) | data formatting | bytes 4194304 | tf_op jit(solution)/shard_map/cbk,bgkl->bcgl/dot_general | solution.py:44
  3.1 0.8 select_reduce_fusion
  3.9 2.5 %copy.56 = f32[128,8,512]{2,0,1:T(8,128)} copy(f32[128,8,512]{2,1,0:T(8,128)S(1)} %bitcast.91) | data formatting | bytes 4194304 | tf_op jit(solution)/shard_map/reshape;reshape | solution.py:51
  6.5 5.9 %all-to-all-start = ((f32[128,8,512]{2,0,1:T(8,128)}), f32[128,8,512]{2,0,1:T(8,128)}, u32[]{:S(2)}, u32[]{:S(2)}) async-start(f32[128,8,512]{2,0,1:T(8,128)} %copy.56), calls=%async_computation | async-start | bytes 4194304 | tf_op jit(solution)/shard_map/all_to_all | solution.py:53
  13.1 51.8 %psum.7 = f32[8,16]{1,0:T(8,128)S(1)} all-reduce(f32[8,16]{1,0:T(8,128)S(1)} %mul.54), channel_id=1, replica_groups=mesh['slab'=4,'modes'=8] {'modes'}, use_global_device_ids=true, to_apply=%region_3.4 | all-reduce | flops 128 | bytes 1024 | tf_op jit(solution)/shard_map/psum | solution.py:58
  64.9 0.8 dynamic-slice_bitcast_fusion
  65.7 1.8 %reduce_sum.30 = f32[128,512]{1,0:T(8,128)S(1)} reduce(f32[128,8,512]{2,0,1:T(8,128)} %all-to-all-done, f32[]{:T(128)} %constant.20.clone.1), dimensions={1}, to_apply=%region_1.2 | reduce | flops 458752 | bytes 2359300 | tf_op jit(solution)/shard_map/reduce_sum | solution.py:24
  67.8 12.1 %while.28 = (s32[]{:T(128)}, f32[16,4,128]{2,0,1:T(8,128)S(1)}, f32[4,128,128]{2,1,0:T(8,128)S(1)}, f32[8,16,4,128]{3,1,2,0:T(8,128)S(1)}, f32[8,4,128,128]{3,2,...) while((s32[]{:T(128)}, f32[16,4,128]{2,0,1:T(8,128)S(1)}, ...), condition=%wide.region_5.6_spmd, body=%wide.region_4.5_spmd.sunk | while | flops 113262592 | bytes 2297445 | solution.py:84
  68.2 0.7 bitcast_dynamic-update-slice_fusion.5
  68.9 0.4 fusion.47
  69.3 0.3 bitcast_dynamic-update-slice_fusion.4
  69.7 0.7 bitcast_dynamic-update-slice_fusion.5
  70.4 0.4 fusion.47
  71.2 0.7 bitcast_dynamic-update-slice_fusion.5
  71.9 0.4 fusion.47
  72.3 0.3 bitcast_dynamic-update-slice_fusion.4
  72.7 0.7 bitcast_dynamic-update-slice_fusion.5
  73.4 0.4 fusion.47
  74.2 0.7 bitcast_dynamic-update-slice_fusion.5
  75.0 0.4 fusion.47
  75.4 0.3 bitcast_dynamic-update-slice_fusion.4
  75.7 0.7 bitcast_dynamic-update-slice_fusion.5
  76.5 0.4 fusion.47
  77.2 0.7 bitcast_dynamic-update-slice_fusion.5
  78.0 0.4 fusion.47
  78.8 0.7 bitcast_dynamic-update-slice_fusion.5
  79.5 0.4 fusion.47
  79.9 1.0 slice_bitcast_fusion
  80.9 29.3 %while.29 = (s32[]{:T(128)}, f32[16,4,128]{2,0,1:T(8,128)S(1)}, f32[16,4,128]{2,0,1:T(8,128)S(1)}, pred[]{:T(512)}, f32[4,128,128]{2,1,0:T(8,128)S(1)}, /*index=...) while((s32[]{:T(128)}, f32[16,4,128]{2,0,1:T(8,128)S(1)}, ...), condition=%wide.region_7.8_spmd, body=%wide.region_6.7_spmd.sunk | while | flops 25198592 | bytes 1179831 | solution.py:107
  80.9 0.3 fusion.52
  81.2 7.7 %collective-permute-start = (f32[16,4,128]{2,0,1:T(8,128)S(1)}, f32[16,4,128]{2,0,1:T(8,128)S(1)}, u32[]{:S(2)}, u32[]{:S(2)}) collective-permute-start(f32[16,4,128]{2,0,1:T(8,128)S(1)} %fusion.52), channel_id=1, source_target_pairs={{0,8},{8,16},{16,24},{1,9},{9,17},{17,25},{2,10},{10,18},{18,26},{... | collective-permute-start | bytes 98312 | tf_op jit(solution)/shard_map/while/body/eval_jaxpr/ppermute | solution.py:13
  89.0 0.3 fusion.53
  89.3 1.9 %collective-permute-start.1 = (f32[16,4,128]{2,0,1:T(8,128)S(1)}, f32[16,4,128]{2,0,1:T(8,128)S(1)}, u32[]{:S(2)}, u32[]{:S(2)}) collective-permute-start(f32[16,4,128]{2,0,1:T(8,128)S(1)} %fusion.53), channel_id=1, source_target_pairs={{8,0},{16,8},{24,16},{9,1},{17,9},{25,17},{10,2},{18,10},{26,18},{... | collective-permute-start | bytes 98312 | tf_op jit(solution)/shard_map/while/body/eval_jaxpr/ppermute | solution.py:13
  91.2 3.3 %collective-permute-done.1 = f32[16,4,128]{2,0,1:T(8,128)S(1)} collective-permute-done((f32[16,4,128]{2,0,1:T(8,128)S(1)}, f32[16,4,128]{2,0,1:T(8,128)S(1)}, u32[]{:S(2)}, u32[]{:S(2)}) %collective-permute-start.1) | collective-permute-done | bytes 32800 | tf_op jit(solution)/shard_map/while/body/eval_jaxpr/ppermute | solution.py:13
  94.5 0.3 fusion.52
  94.9 1.9 %collective-permute-start = (f32[16,4,128]{2,0,1:T(8,128)S(1)}, f32[16,4,128]{2,0,1:T(8,128)S(1)}, u32[]{:S(2)}, u32[]{:S(2)}) collective-permute-start(f32[16,4,128]{2,0,1:T(8,128)S(1)} %fusion.52), channel_id=1, source_target_pairs={{0,8},{8,16},{16,24},{1,9},{9,17},{17,25},{2,10},{10,18},{18,26},{... | collective-permute-start | bytes 98312 | tf_op jit(solution)/shard_map/while/body/eval_jaxpr/ppermute | solution.py:13
  96.8 0.3 fusion.53
  97.1 2.4 %collective-permute-start.1 = (f32[16,4,128]{2,0,1:T(8,128)S(1)}, f32[16,4,128]{2,0,1:T(8,128)S(1)}, u32[]{:S(2)}, u32[]{:S(2)}) collective-permute-start(f32[16,4,128]{2,0,1:T(8,128)S(1)} %fusion.53), channel_id=1, source_target_pairs={{8,0},{16,8},{24,16},{9,1},{17,9},{25,17},{10,2},{18,10},{26,18},{... | collective-permute-start | bytes 98312 | tf_op jit(solution)/shard_map/while/body/eval_jaxpr/ppermute | solution.py:13
  99.6 2.8 %collective-permute-done.1 = f32[16,4,128]{2,0,1:T(8,128)S(1)} collective-permute-done((f32[16,4,128]{2,0,1:T(8,128)S(1)}, f32[16,4,128]{2,0,1:T(8,128)S(1)}, u32[]{:S(2)}, u32[]{:S(2)}) %collective-permute-start.1) | collective-permute-done | bytes 32800 | tf_op jit(solution)/shard_map/while/body/eval_jaxpr/ppermute | solution.py:13
  102.4 0.3 fusion.52
  102.7 1.9 %collective-permute-start = (f32[16,4,128]{2,0,1:T(8,128)S(1)}, f32[16,4,128]{2,0,1:T(8,128)S(1)}, u32[]{:S(2)}, u32[]{:S(2)}) collective-permute-start(f32[16,4,128]{2,0,1:T(8,128)S(1)} %fusion.52), channel_id=1, source_target_pairs={{0,8},{8,16},{16,24},{1,9},{9,17},{17,25},{2,10},{10,18},{18,26},{... | collective-permute-start | bytes 98312 | tf_op jit(solution)/shard_map/while/body/eval_jaxpr/ppermute | solution.py:13
  104.6 0.3 fusion.53
  105.0 2.4 %collective-permute-start.1 = (f32[16,4,128]{2,0,1:T(8,128)S(1)}, f32[16,4,128]{2,0,1:T(8,128)S(1)}, u32[]{:S(2)}, u32[]{:S(2)}) collective-permute-start(f32[16,4,128]{2,0,1:T(8,128)S(1)} %fusion.53), channel_id=1, source_target_pairs={{8,0},{16,8},{24,16},{9,1},{17,9},{25,17},{10,2},{18,10},{26,18},{... | collective-permute-start | bytes 98312 | tf_op jit(solution)/shard_map/while/body/eval_jaxpr/ppermute | solution.py:13
  107.4 2.8 %collective-permute-done.1 = f32[16,4,128]{2,0,1:T(8,128)S(1)} collective-permute-done((f32[16,4,128]{2,0,1:T(8,128)S(1)}, f32[16,4,128]{2,0,1:T(8,128)S(1)}, u32[]{:S(2)}, u32[]{:S(2)}) %collective-permute-start.1) | collective-permute-done | bytes 32800 | tf_op jit(solution)/shard_map/while/body/eval_jaxpr/ppermute | solution.py:13
  110.2 2.8 %fusion.12 = f32[8,16,4,128]{3,1,0,2:T(8,128)S(1)} fusion(f32[8,4,128,128]{3,2,1,0:T(8,128)} %get-tuple-element.102, f32[8,16,4,128]{3,1,2,0:T(8,128)S(1)} %get-tuple-element.101, f32[16,4,128]{2,0,1:T(8,128)S(1)} %get-tuple-element.103, f32[16,4,128]{2,0,1:T(8,128)S(1)} %get-tuple-element.104, pred[4]{0:T(512)(128)(4,1)S(1)} %broadcast_compare_fusion), kind=kOutput, calls=%fused_computation.18 | convolution fusion | flops 100737024 | bytes 2686980 | tf_op jit(solution)/shard_map/ybk,xbkl->xybl/dot_general | solution.py:109
  113.3 0.7 copy.87
  (68 shorter events, 3.3 us)
Async XLA Ops:
  0.0 1.4 %copy-start = (bf16[4,8,128,128]{3,2,1,0:T(8,128)(2,1)S(1)}, bf16[4,8,128,128]{3,2,1,0:T(8,128)(2,1)}, u32[]{:S(2)}) copy-start(bf16[4,8,128,128]{3,2,1,0:T(8,128)(2,1)} %param.16) | copy-start | bytes 3145732
  1.8 1.2 %copy-start.3 = (s32[4,8]{1,0:T(4,128)S(1)}, s32[4,8]{1,0:T(4,128)}, u32[]{:S(2)}) copy-start(s32[4,8]{1,0:T(4,128)} %param.17) | copy-start | bytes 388
  6.4 6.0 %copy-start.1 = (f32[4,128,128]{2,1,0:T(8,128)S(1)}, f32[4,128,128]{2,1,0:T(8,128)}, u32[]{:S(2)}) copy-start(f32[4,128,128]{2,1,0:T(8,128)} %param.22) | copy-start | bytes 786436
  6.4 6.0 %copy-start.2 = (f32[512]{0:T(512)S(1)}, f32[512]{0:T(512)}, u32[]{:S(2)}) copy-start(f32[512]{0:T(512)} %param.21) | copy-start | bytes 6148
  6.4 6.2 %copy-start.4 = (f32[4,512]{1,0:T(4,128)S(1)}, f32[4,512]{1,0:T(4,128)}, u32[]{:S(2)}) copy-start(f32[4,512]{1,0:T(4,128)} %param.24) | copy-start | bytes 24580
  6.4 6.2 %copy-start.6 = (s32[16]{0:T(128)S(1)}, s32[16]{0:T(128)}, u32[]{:S(2)}) copy-start(s32[16]{0:T(128)} %param.25) | copy-start | bytes 196
  6.4 6.4 %copy-start.5 = (f32[4,512]{1,0:T(4,128)S(1)}, f32[4,512]{1,0:T(4,128)}, u32[]{:S(2)}) copy-start(f32[4,512]{1,0:T(4,128)} %param.23) | copy-start | bytes 24580
  6.4 59.2 %copy-start.7 = (s32[4]{0:T(128)S(1)}, s32[4]{0:T(128)}, u32[]{:S(2)}) copy-start(s32[4]{0:T(128)} %param.20) | copy-start | bytes 52
  6.5 59.2 %all-to-all-start = ((f32[128,8,512]{2,0,1:T(8,128)}), f32[128,8,512]{2,0,1:T(8,128)}, u32[]{:S(2)}, u32[]{:S(2)}) async-start(f32[128,8,512]{2,0,1:T(8,128)} %copy.56), calls=%async_computation | async-start | bytes 4194304 | tf_op jit(solution)/shard_map/all_to_all | solution.py:53
  81.2 10.0 %collective-permute-start = (f32[16,4,128]{2,0,1:T(8,128)S(1)}, f32[16,4,128]{2,0,1:T(8,128)S(1)}, u32[]{:S(2)}, u32[]{:S(2)}) collective-permute-start(f32[16,4,128]{2,0,1:T(8,128)S(1)} %fusion.52), channel_id=1, source_target_pairs={{0,8},{8,16},{16,24},{1,9},{9,17},{17,25},{2,10},{10,18},{18,26},{... | collective-permute-start | bytes 98312 | tf_op jit(solution)/shard_map/while/body/eval_jaxpr/ppermute | solution.py:13
  89.3 5.2 %collective-permute-start.1 = (f32[16,4,128]{2,0,1:T(8,128)S(1)}, f32[16,4,128]{2,0,1:T(8,128)S(1)}, u32[]{:S(2)}, u32[]{:S(2)}) collective-permute-start(f32[16,4,128]{2,0,1:T(8,128)S(1)} %fusion.53), channel_id=1, source_target_pairs={{8,0},{16,8},{24,16},{9,1},{17,9},{25,17},{10,2},{18,10},{26,18},{... | collective-permute-start | bytes 98312 | tf_op jit(solution)/shard_map/while/body/eval_jaxpr/ppermute | solution.py:13
  94.9 4.7 %collective-permute-start = (f32[16,4,128]{2,0,1:T(8,128)S(1)}, f32[16,4,128]{2,0,1:T(8,128)S(1)}, u32[]{:S(2)}, u32[]{:S(2)}) collective-permute-start(f32[16,4,128]{2,0,1:T(8,128)S(1)} %fusion.52), channel_id=1, source_target_pairs={{0,8},{8,16},{16,24},{1,9},{9,17},{17,25},{2,10},{10,18},{18,26},{... | collective-permute-start | bytes 98312 | tf_op jit(solution)/shard_map/while/body/eval_jaxpr/ppermute | solution.py:13
  97.1 5.2 %collective-permute-start.1 = (f32[16,4,128]{2,0,1:T(8,128)S(1)}, f32[16,4,128]{2,0,1:T(8,128)S(1)}, u32[]{:S(2)}, u32[]{:S(2)}) collective-permute-start(f32[16,4,128]{2,0,1:T(8,128)S(1)} %fusion.53), channel_id=1, source_target_pairs={{8,0},{16,8},{24,16},{9,1},{17,9},{25,17},{10,2},{18,10},{26,18},{... | collective-permute-start | bytes 98312 | tf_op jit(solution)/shard_map/while/body/eval_jaxpr/ppermute | solution.py:13
  102.7 4.7 %collective-permute-start = (f32[16,4,128]{2,0,1:T(8,128)S(1)}, f32[16,4,128]{2,0,1:T(8,128)S(1)}, u32[]{:S(2)}, u32[]{:S(2)}) collective-permute-start(f32[16,4,128]{2,0,1:T(8,128)S(1)} %fusion.52), channel_id=1, source_target_pairs={{0,8},{8,16},{16,24},{1,9},{9,17},{17,25},{2,10},{10,18},{18,26},{... | collective-permute-start | bytes 98312 | tf_op jit(solution)/shard_map/while/body/eval_jaxpr/ppermute | solution.py:13
  105.0 5.2 %collective-permute-start.1 = (f32[16,4,128]{2,0,1:T(8,128)S(1)}, f32[16,4,128]{2,0,1:T(8,128)S(1)}, u32[]{:S(2)}, u32[]{:S(2)}) collective-permute-start(f32[16,4,128]{2,0,1:T(8,128)S(1)} %fusion.53), channel_id=1, source_target_pairs={{8,0},{16,8},{24,16},{9,1},{17,9},{25,17},{10,2},{18,10},{26,18},{... | collective-permute-start | bytes 98312 | tf_op jit(solution)/shard_map/while/body/eval_jaxpr/ppermute | solution.py:13
where the time goes:
time: 114 us
  blocking collectives  51.8 us (45%)
  starting transfers between devices  24.1 us (21%)
  local copies, waits for them, and re-layouts  12.7 us (11%)
  matrix products  11.5 us (10%)
  waiting for transfers between devices  8.88 us (8%)
  other arithmetic  4.31 us (4%)
    psum x1, blocking collectives, per_device(): pseudo_warmth_sum = lax.psum(branch_pseudo_warmth, 'modes')  51.8 us
    ppermute x6, starting transfers between devices, shifted(): return lax.ppermute(block, axis, route)  18.2 us
    ppermute x6, waiting for transfers between devices, shifted(): return lax.ppermute(block, axis, route)  8.88 us
    all_to_all x1, starting transfers between devices, per_device(): lax.all_to_all(sectioned, 'modes', split_axis=1, concat_axis=1, tiled=True)  5.86 us
    dynamic_update_slice x8, local copies, waits for them, and re-layouts, per_device(): _, (particular, powers) = lax.scan(local_sweep, start_carry, ordered)  5.79 us
    dot_general x8, matrix products, local_sweep(): jnp.einsum('bkl,blm->bkm', power_matrix, step_matrix, precision=lax.Preci...  3.13 us
    dot_general x1, matrix products, per_device(): jnp.einsum('ybk,xbkl->xybl', inflow, powers, precision=lax.Precision.HIGH...  2.79 us
    dot_general x8, matrix products, local_sweep(): jnp.einsum('ybk,bkl->ybl', layer_source + rate_table * previous, transfer...  2.71 us
  transfers between devices with their start and end apart: 7, of which 3 were waited for; matrix products, arithmetic and copies ran while one was open for 2% of the time, Pallas kernels for 0%

commit v1 on v0

--- a/solution.py
+++ b/solution.py
@@ -1,10 +1,16 @@
+import functools
+
 import jax
 import jax.numpy as jnp
 from jax import lax
+from jax.experimental import pallas as pl
+from jax.experimental.pallas import tpu as pltpu
 from jax.sharding import PartitionSpec as P
 
 BLK = 128
 SHELL = 4
+MESH = pl.DeviceIdType.MESH
+KERNEL_BUFFER_BYTES = 24 * 2**20
 
 
 def shifted(block, axis, distance):
@@ -24,7 +30,7 @@
     return jnp.sum(pieces, axis=1)
 
 
-def per_device(
+def per_device_plain(
     occupation_prior,
     coupling,
     pattern,
@@ -113,6 +119,394 @@
     return result.reshape(cell_count, local_width)
 
 
+def halves(matrix):
+    high = matrix.astype(jnp.bfloat16)
+    return high, (matrix - high.astype(jnp.float32)).astype(jnp.bfloat16)
+
+
+def product(left, right_high, right_low):
+    left_high, left_low = halves(left)
+    dot = functools.partial(jnp.dot, preferred_element_type=jnp.float32)
+    return dot(left_high, right_high) + (dot(left_high, right_low) + dot(left_low, right_high))
+
+
+def visiting_order(z, count):
+    right = list(range(count - 1, z, -1))
+    left = list(range(z))
+    return (right + left if 2 * z < count else left + right) + [z]
+
+
+def kernel(
+    lines,
+    slabs,
+    occupation,
+    coupling,
+    pattern,
+    weights,
+    slope,
+    direction,
+    rate,
+    inscatter,
+    inflow_low,
+    inflow_high,
+    front,
+    out,
+    held,
+    part,
+    from_mate,
+    from_left,
+    from_right,
+    source,
+    local,
+    wall_part,
+    walls,
+    faces,
+    scatter_high,
+    scatter_low,
+    power_high,
+    power_low,
+    coupling_sem,
+    mate_send,
+    mate_recv,
+    line_send,
+    left_recv,
+    right_recv,
+    face_send,
+    face_recv,
+):
+    cells, width = occupation.shape
+    lateral = front.shape[0]
+    layers = cells // lateral
+    piece = cells // 2
+    me = lax.axis_index("modes")
+    slab = lax.axis_index("slab")
+    z, y = lax.div(me, 2), lax.rem(me, 2)
+    mate = 2 * z + 1 - y
+
+    orders = [visiting_order(at, lines) for at in range(lines)]
+
+    def in_order(step):
+        spot = jnp.int32(orders[0][step])
+        for at in range(1, lines):
+            spot = jnp.where(z == at, jnp.int32(orders[at][step]), spot)
+        return spot
+
+    places = [in_order(step) for step in range(lines)]
+    destinations = [2 * place + 1 - y for place in places] + [2 * place + y for place in places]
+
+    def fetch(group):
+        return pltpu.make_async_copy(coupling.at[:, group], held.at[group], coupling_sem.at[group])
+
+    for group in destinations:
+        fetch(group).start()
+
+    barrier = pltpu.get_barrier_semaphore()
+    pl.semaphore_signal(barrier, inc=1, device_id={"modes": mate}, device_id_type=MESH)
+
+    @pl.when(z > 0)
+    def _():
+        pl.semaphore_signal(barrier, inc=1, device_id={"modes": me - 2}, device_id_type=MESH)
+
+    @pl.when(z < lines - 1)
+    def _():
+        pl.semaphore_signal(barrier, inc=1, device_id={"modes": me + 2}, device_id_type=MESH)
+
+    for away in range(1, slabs):
+        pl.semaphore_signal(
+            barrier,
+            inc=1,
+            device_id={"slab": lax.rem(slab + away, slabs)},
+            device_id_type=MESH,
+        )
+
+    prior = occupation[...]
+    rounded = prior.astype(jnp.bfloat16)
+    warmth = jnp.sum(prior * weights[...], axis=1, keepdims=True)
+
+    def make_part(group):
+        fetch(group).wait()
+        rows = []
+        for block in range(SHELL):
+            table = held[group, block]
+            fed = pattern[block, group]
+            rows.append(
+                jnp.concatenate(
+                    [
+                        jnp.where(fed == spot, table, jnp.zeros_like(table))
+                        for spot in range(SHELL)
+                    ],
+                    axis=1,
+                )
+            )
+        chosen = jnp.concatenate(rows, axis=0)
+        offset = pl.multiple_of(group * width, width)
+        part[group] = (
+            jnp.dot(rounded, chosen, preferred_element_type=jnp.float32)
+            + warmth * slope[:, pl.ds(offset, width)]
+        )
+
+    def rows_of(half):
+        return pl.ds(half * piece, piece)
+
+    def mate_copy(place, half):
+        return pltpu.make_async_remote_copy(
+            src_ref=part.at[2 * place + 1 - y, rows_of(half)],
+            dst_ref=from_mate.at[place, rows_of(half)],
+            send_sem=mate_send.at[place, half],
+            recv_sem=mate_recv.at[place, half],
+            device_id={"modes": mate},
+            device_id_type=MESH,
+        )
+
+    def line_copy(place, half, step):
+        return pltpu.make_async_remote_copy(
+            src_ref=part.at[2 * place + y, rows_of(half)],
+            dst_ref=(from_left if step > 0 else from_right).at[place, rows_of(half)],
+            send_sem=line_send.at[place, half],
+            recv_sem=(left_recv if step > 0 else right_recv).at[place, half],
+            device_id={"modes": me + 2 * step},
+            device_id_type=MESH,
+        )
+
+    make_part(destinations[0])
+    pl.semaphore_wait(
+        barrier, slabs + (z > 0).astype(jnp.int32) + (z < lines - 1).astype(jnp.int32)
+    )
+    for half in range(2):
+        mate_copy(places[0], half).start()
+    for group in destinations[1:]:
+        make_part(group)
+
+    row_id = lax.broadcasted_iota(jnp.int32, (BLK, BLK), 0)
+    column_id = lax.broadcasted_iota(jnp.int32, (BLK, BLK), 1)
+    for row in range(lateral):
+        pick = pl.ds(front[row], 1)
+        walls[0, pl.ds(row, 1)] = inflow_low[pick, :]
+        walls[1, pl.ds(row, 1)] = inflow_high[pick, :]
+
+    def lanes(block):
+        return slice(block * BLK, (block + 1) * BLK)
+
+    def upward(block):
+        return direction[block] == 1
+
+    def rank(block):
+        return jnp.where(upward(block), slab, slabs - 1 - slab)
+
+    for block in range(SHELL):
+        scatter = inscatter[block]
+        scatter_high[block], scatter_low[block] = halves(scatter)
+        diagonal = jnp.where(row_id == column_id, rate[:, lanes(block)], 0.0)
+        matrix = diagonal + jnp.sum(diagonal, axis=1, keepdims=True) * scatter
+        powers = [matrix]
+        while len(powers) < layers:
+            count = len(powers)
+            high, low = halves(powers[-1])
+            fresh = min(count, layers - count)
+            raised = product(jnp.concatenate(powers[:fresh], axis=0), high, low)
+            powers += [raised[at * BLK : (at + 1) * BLK] for at in range(fresh)]
+        for at in range(layers):
+            power_high[block, at], power_low[block, at] = halves(powers[at])
+        carried = jnp.where(upward(block), walls[0, :, lanes(block)], walls[1, :, lanes(block)])
+        for at in range(slabs - 1):
+            moved = product(carried, power_high[block, layers - 1], power_low[block, layers - 1])
+            carried = jnp.where(at < rank(block), moved, carried)
+        wall_part[:, lanes(block)] = carried
+
+    def reduce_at(at):
+        items = [(place, half) for place in orders[at] for half in range(2)]
+        for index, (place, half) in enumerate(items):
+            mate_copy(place, half).wait_recv()
+            if index + 2 < len(items):
+                mate_copy(*items[index + 2]).start()
+            rows = rows_of(half)
+            total = part[2 * place + y, rows] + from_mate[place, rows]
+            if place >= at > 0:
+                line_copy(place, half, 1).wait_recv()
+                total = total + from_left[place, rows]
+            if place <= at < lines - 1:
+                line_copy(place, half, -1).wait_recv()
+                total = total + from_right[place, rows]
+            if place == at:
+                source[rows] = total
+            else:
+                part[2 * place + y, rows] = total
+                line_copy(place, half, 1 if place > at else -1).start()
+
+    for at in range(lines):
+        pl.when(z == at)(functools.partial(reduce_at, at))
+
+    def turned(values):
+        return jnp.concatenate(
+            [values[at * lateral : (at + 1) * lateral] for at in reversed(range(layers))], axis=0
+        )
+
+    for block in range(SHELL):
+        given = source[:, lanes(block)]
+        given = jnp.where(upward(block), given, turned(given))
+        swept = given + product(given, scatter_high[block], scatter_low[block])
+        reach = 1
+        while reach < layers:
+            edge = reach * lateral
+            moved = product(
+                swept[: cells - edge],
+                power_high[block, reach - 1],
+                power_low[block, reach - 1],
+            )
+            swept = jnp.concatenate([swept[:edge], swept[edge:] + moved], axis=0)
+            reach *= 2
+        local[:, lanes(block)] = swept
+        faces[slab, :, lanes(block)] = swept[cells - lateral :]
+
+    def face_copy(away):
+        return pltpu.make_async_remote_copy(
+            src_ref=faces.at[slab],
+            dst_ref=faces.at[slab],
+            send_sem=face_send.at[away - 1],
+            recv_sem=face_recv.at[slab],
+            device_id={"slab": lax.rem(slab + away, slabs)},
+            device_id_type=MESH,
+        )
+
+    for away in range(1, slabs):
+        face_copy(away).start()
+    for away in range(1, slabs):
+        sender = lax.rem(slab + away, slabs)
+        pltpu.make_async_remote_copy(
+            src_ref=faces.at[sender],
+            dst_ref=faces.at[sender],
+            send_sem=face_send.at[away - 1],
+            recv_sem=face_recv.at[sender],
+            device_id={"slab": sender},
+            device_id_type=MESH,
+        ).wait_recv()
+
+    for block in range(SHELL):
+        last_high, last_low = power_high[block, layers - 1], power_low[block, layers - 1]
+        arrived = jnp.zeros((lateral, BLK), jnp.float32)
+        for at in range(slabs - 1):
+            face = jnp.where(
+                upward(block),
+                faces[at, :, lanes(block)],
+                faces[slabs - 1 - at, :, lanes(block)],
+            )
+            moved = face if at == 0 else product(arrived, last_high, last_low) + face
+            arrived = jnp.where(at < rank(block), moved, arrived)
+        inflow = arrived + wall_part[:, lanes(block)]
+        added = jnp.concatenate(
+            [
+                product(inflow, power_high[block, at], power_low[block, at])
+                for at in range(layers)
+            ],
+            axis=0,
+        )
+        swept = local[:, lanes(block)] + added
+        out[:, lanes(block)] = jnp.where(upward(block), swept, turned(swept))
+
+    for place in range(lines):
+        for half in range(2):
+            mate_copy(place, half).wait_send()
+
+    def finish_at(at):
+        for place in range(lines):
+            if place != at:
+                for half in range(2):
+                    line_copy(place, half, 1 if place > at else -1).wait_send()
+
+    for at in range(lines):
+        pl.when(z == at)(functools.partial(finish_at, at))
+    for away in range(1, slabs):
+        face_copy(away).wait_send()
+
+
+def per_device(
+    occupation_prior,
+    coupling,
+    pattern,
+    pseudo_weights,
+    equilibrium_slope,
+    direction,
+    stream_rate,
+    inscatter,
+    inflow_low,
+    inflow_high,
+    front_of_row,
+):
+    cells, width = occupation_prior.shape
+    groups = lax.axis_size("modes")
+    slabs = lax.axis_size("slab")
+    lines = groups // 2
+    lateral = front_of_row.shape[0]
+    layers = cells // lateral
+    block_bytes = 4 * cells * width
+    needed = block_bytes * (groups + 3 * lines) + 2 * coupling.size
+    if groups % 2 or layers & (layers - 1) or needed > KERNEL_BUFFER_BYTES:
+        return per_device_plain(
+            occupation_prior,
+            coupling,
+            pattern,
+            pseudo_weights,
+            equilibrium_slope,
+            direction,
+            stream_rate,
+            inscatter,
+            inflow_low,
+            inflow_high,
+            front_of_row,
+        )
+    vmem = pl.BlockSpec(memory_space=pltpu.VMEM)
+    smem = pl.BlockSpec(memory_space=pltpu.SMEM)
+    far = pl.BlockSpec(memory_space=pl.ANY)
+    f32, bf16 = jnp.float32, jnp.bfloat16
+    dma = pltpu.SemaphoreType.DMA
+    return pl.pallas_call(
+        functools.partial(kernel, lines, slabs),
+        out_shape=jax.ShapeDtypeStruct((cells, width), f32),
+        in_specs=[vmem, far, smem, vmem, vmem, smem, vmem, vmem, vmem, vmem, smem],
+        out_specs=vmem,
+        scratch_shapes=[
+            pltpu.VMEM((groups, SHELL, BLK, BLK), bf16),
+            pltpu.VMEM((groups, cells, width), f32),
+            pltpu.VMEM((lines, cells, width), f32),
+            pltpu.VMEM((lines, cells, width), f32),
+            pltpu.VMEM((lines, cells, width), f32),
+            pltpu.VMEM((cells, width), f32),
+            pltpu.VMEM((cells, width), f32),
+            pltpu.VMEM((lateral, width), f32),
+            pltpu.VMEM((2, lateral, width), f32),
+            pltpu.VMEM((slabs, lateral, width), f32),
+            pltpu.VMEM((SHELL, BLK, BLK), bf16),
+            pltpu.VMEM((SHELL, BLK, BLK), bf16),
+            pltpu.VMEM((SHELL, layers, BLK, BLK), bf16),
+            pltpu.VMEM((SHELL, layers, BLK, BLK), bf16),
+            dma((groups,)),
+            dma((lines, 2)),
+            dma((lines, 2)),
+            dma((lines, 2)),
+            dma((lines, 2)),
+            dma((lines, 2)),
+            dma((max(slabs - 1, 1),)),
+            dma((slabs,)),
+        ],
+        compiler_params=pltpu.CompilerParams(
+            collective_id=0, has_side_effects=True, vmem_limit_bytes=56 * 2**20
+        ),
+        name="sweep",
+    )(
+        occupation_prior,
+        coupling,
+        pattern,
+        pseudo_weights.reshape(1, width),
+        equilibrium_slope.reshape(1, groups * width),
+        direction,
+        stream_rate.reshape(1, width),
+        inscatter,
+        inflow_low,
+        inflow_high,
+        front_of_row,
+    )
+
+
 def solution(mesh):
     placed = (
         P("slab", "modes"),

time: 114 us -> 40.7 us (0.36)
  the two profiles are of different devices: /device:TPU:9 before, /device:TPU:0 now
where the time goes in v1:
time: 40.7 us; the launch traced here: 40.6 us
  Pallas kernels  38.9 us (96%)
  local copies, waits for them, and re-layouts  1.67 us (4%)
    pallas_call x1, Pallas kernels, per_device(): pl.pallas_call(functools.partial(kernel, lines, slabs), out_shape=jax.Sha...  38.9 us
    unnamed x1, local copies, waits for them, and re-layouts  1.67 us

profile of v1, /device:TPU:0, one launch (start us, length us, event | category | flops | bytes accessed | tf_op | source)
XLA Modules:
  0.0 40.6 jit_solution(10377614531491394267)
XLA Ops:
  0.0 38.9 %sweep.1 = f32[128,512]{1,0:T(8,128)} custom-call(f32[128,512]{1,0:T(8,128)} %occupation.1, bf16[4,8,128,128]{3,2,1,0:T(8,128)(2,1)} %coupling.1, s32[4,8]{1,0:T(4,128)} %pattern.1, f32[1,512]{1,0:T(1,128)} %bitcast.4, f32[1,4096]{1,0:T(1,128)} %bitcast.3, s32[4]{0:T(128)} %direction.1, f32[1,512]{1,0:T(1,128)} %bitcast.5, f32[4,128,128]{2,1,0:T(8,128)} %inscatter.1, ...), custom_call_target="tpu_custom_call" | custom-call | tf_op jit(solution)/shard_map/sweep/pallas_call | solution.py:462
  38.9 1.7 %copy.13 = f32[128,512]{1,0:T(8,128)} copy(f32[128,512]{1,0:T(8,128)} %sweep.1) | data formatting | bytes 524288

commit v2 on v1

--- a/solution.py
+++ b/solution.py
@@ -124,10 +124,23 @@
     return high, (matrix - high.astype(jnp.float32)).astype(jnp.bfloat16)
 
 
-def product(left, right_high, right_low):
-    left_high, left_low = halves(left)
-    dot = functools.partial(jnp.dot, preferred_element_type=jnp.float32)
-    return dot(left_high, right_high) + (dot(left_high, right_low) + dot(left_low, right_high))
+def packed(matrix):
+    high, low = halves(matrix)
+    return jnp.concatenate(
+        [
+            jnp.concatenate([high, low], axis=1),
+            jnp.concatenate([high, jnp.zeros_like(low)], axis=1),
+        ],
+        axis=0,
+    )
+
+
+def product(left, right):
+    terms = jnp.dot(
+        jnp.concatenate(halves(left), axis=1), right, preferred_element_type=jnp.float32
+    )
+    width = terms.shape[1] // 2
+    return terms[:, :width] + terms[:, width:]
 
 
 def visiting_order(z, count):
@@ -161,10 +174,9 @@
     wall_part,
     walls,
     faces,
-    scatter_high,
-    scatter_low,
-    power_high,
-    power_low,
+    scatter_table,
+    power_table,
+    leap_table,
     coupling_sem,
     mate_send,
     mate_recv,
@@ -274,8 +286,11 @@
     )
     for half in range(2):
         mate_copy(places[0], half).start()
-    for group in destinations[1:]:
-        make_part(group)
+    for step in range(1, len(destinations)):
+        make_part(destinations[step])
+        if step == 1:
+            for half in range(2):
+                mate_copy(places[1], half).start()
 
     row_id = lax.broadcasted_iota(jnp.int32, (BLK, BLK), 0)
     column_id = lax.broadcasted_iota(jnp.int32, (BLK, BLK), 1)
@@ -293,32 +308,37 @@
     def rank(block):
         return jnp.where(upward(block), slab, slabs - 1 - slab)
 
-    for block in range(SHELL):
+    def prepare(block):
         scatter = inscatter[block]
-        scatter_high[block], scatter_low[block] = halves(scatter)
+        scatter_table[block] = packed(scatter)
         diagonal = jnp.where(row_id == column_id, rate[:, lanes(block)], 0.0)
         matrix = diagonal + jnp.sum(diagonal, axis=1, keepdims=True) * scatter
-        powers = [matrix]
+        powers, tables = [matrix], [packed(matrix)]
         while len(powers) < layers:
             count = len(powers)
-            high, low = halves(powers[-1])
             fresh = min(count, layers - count)
-            raised = product(jnp.concatenate(powers[:fresh], axis=0), high, low)
+            raised = product(jnp.concatenate(powers[:fresh], axis=0), tables[-1])
             powers += [raised[at * BLK : (at + 1) * BLK] for at in range(fresh)]
+            tables += [packed(power) for power in powers[count:]]
         for at in range(layers):
-            power_high[block, at], power_low[block, at] = halves(powers[at])
+            power_table[block, at] = tables[at]
+        leap = powers[-1]
+        for at in range(slabs - 2):
+            leap_table[block, at] = packed(leap)
+            leap = product(leap, tables[-1])
         carried = jnp.where(upward(block), walls[0, :, lanes(block)], walls[1, :, lanes(block)])
         for at in range(slabs - 1):
-            moved = product(carried, power_high[block, layers - 1], power_low[block, layers - 1])
-            carried = jnp.where(at < rank(block), moved, carried)
+            carried = jnp.where(at < rank(block), product(carried, tables[-1]), carried)
         wall_part[:, lanes(block)] = carried
 
-    def reduce_at(at):
+    def reduce_at(at, first, last):
         items = [(place, half) for place in orders[at] for half in range(2)]
-        for index, (place, half) in enumerate(items):
+        for index, (place, half) in enumerate(items[:last]):
+            if index < first:
+                continue
             mate_copy(place, half).wait_recv()
-            if index + 2 < len(items):
-                mate_copy(*items[index + 2]).start()
+            if index + 4 < len(items):
+                mate_copy(*items[index + 4]).start()
             rows = rows_of(half)
             total = part[2 * place + y, rows] + from_mate[place, rows]
             if place >= at > 0:
@@ -333,8 +353,12 @@
                 part[2 * place + y, rows] = total
                 line_copy(place, half, 1 if place > at else -1).start()
 
-    for at in range(lines):
-        pl.when(z == at)(functools.partial(reduce_at, at))
+    edges = [0, 1, 2, 3, 4, 2 * lines]
+    for step in range(len(edges) - 1):
+        for at in range(lines):
+            pl.when(z == at)(functools.partial(reduce_at, at, edges[step], edges[step + 1]))
+        if step < SHELL:
+            prepare(step)
 
     def turned(values):
         return jnp.concatenate(
@@ -344,15 +368,11 @@
     for block in range(SHELL):
         given = source[:, lanes(block)]
         given = jnp.where(upward(block), given, turned(given))
-        swept = given + product(given, scatter_high[block], scatter_low[block])
+        swept = given + product(given, scatter_table[block])
         reach = 1
         while reach < layers:
             edge = reach * lateral
-            moved = product(
-                swept[: cells - edge],
-                power_high[block, reach - 1],
-                power_low[block, reach - 1],
-            )
+            moved = product(swept[: cells - edge], power_table[block, reach - 1])
             swept = jnp.concatenate([swept[:edge], swept[edge:] + moved], axis=0)
             reach *= 2
         local[:, lanes(block)] = swept
@@ -382,20 +402,25 @@
         ).wait_recv()
 
     for block in range(SHELL):
-        last_high, last_low = power_high[block, layers - 1], power_low[block, layers - 1]
         arrived = jnp.zeros((lateral, BLK), jnp.float32)
-        for at in range(slabs - 1):
-            face = jnp.where(
-                upward(block),
-                faces[at, :, lanes(block)],
-                faces[slabs - 1 - at, :, lanes(block)],
-            )
-            moved = face if at == 0 else product(arrived, last_high, last_low) + face
-            arrived = jnp.where(at < rank(block), moved, arrived)
+        for away in range(slabs - 1):
+            sender = rank(block) - 1 - away
+            face = jnp.zeros((lateral, BLK), jnp.float32)
+            for at in range(slabs - 1):
+                face = jnp.where(
+                    sender == at,
+                    jnp.where(
+                        upward(block),
+                        faces[at, :, lanes(block)],
+                        faces[slabs - 1 - at, :, lanes(block)],
+                    ),
+                    face,
+                )
+            arrived += product(face, leap_table[block, away - 1]) if away else face
         inflow = arrived + wall_part[:, lanes(block)]
         added = jnp.concatenate(
             [
-                product(inflow, power_high[block, at], power_low[block, at])
+                product(inflow, power_table[block, at])
                 for at in range(layers)
             ],
             axis=0,
@@ -475,10 +500,9 @@
             pltpu.VMEM((lateral, width), f32),
             pltpu.VMEM((2, lateral, width), f32),
             pltpu.VMEM((slabs, lateral, width), f32),
-            pltpu.VMEM((SHELL, BLK, BLK), bf16),
-            pltpu.VMEM((SHELL, BLK, BLK), bf16),
-            pltpu.VMEM((SHELL, layers, BLK, BLK), bf16),
-            pltpu.VMEM((SHELL, layers, BLK, BLK), bf16),
+            pltpu.VMEM((SHELL, 2 * BLK, 2 * BLK), bf16),
+            pltpu.VMEM((SHELL, layers, 2 * BLK, 2 * BLK), bf16),
+            pltpu.VMEM((SHELL, max(slabs - 2, 1), 2 * BLK, 2 * BLK), bf16),
             dma((groups,)),
             dma((lines, 2)),
             dma((lines, 2)),
@@ -489,7 +513,7 @@
             dma((slabs,)),
         ],
         compiler_params=pltpu.CompilerParams(
-            collective_id=0, has_side_effects=True, vmem_limit_bytes=56 * 2**20
+            collective_id=0, has_side_effects=True, vmem_limit_bytes=53 * 2**20
         ),
         name="sweep",
     )(

time: 40.7 us -> 42.8 us (1.052)
  local copies, waits for them, and re-layouts: 1.67 us -> 6.09 us
  Pallas kernels: 38.9 us -> 36.3 us
    unnamed x1 -> x21, local copies, waits for them, and re-layouts: 1.67 us -> 6.09 us
    pallas_call x1, Pallas kernels: 38.9 us -> 36.3 us  [per_device(): pl.pallas_call(functools.partial(kernel, lines, slabs), out_shape=jax.Sha...]
where the time goes in v2:
time: 42.8 us; the launch traced here: 42.4 us
  Pallas kernels  36.3 us (85%)
  local copies, waits for them, and re-layouts  6.09 us (14%)
    pallas_call x1, Pallas kernels, per_device(): pl.pallas_call(functools.partial(kernel, lines, slabs), out_shape=jax.Sha...  36.3 us
    unnamed x21, local copies, waits for them, and re-layouts  6.09 us

profile of v2, /device:TPU:0, one launch (start us, length us, event | category | flops | bytes accessed | tf_op | source)
XLA Modules:
  0.0 42.4 jit_solution(7035278144066913932)
XLA Ops:
  0.0 0.0 copy-start.6
  0.0 0.0 copy-start.5
  0.0 0.0 copy-start.8
  0.0 0.0 copy-start.9
  0.0 0.7 %copy-done.6 = f32[512]{0:T(512)S(1)} copy-done((f32[512]{0:T(512)S(1)}, f32[512]{0:T(512)}, u32[]{:S(2)}) %copy-start.6) | copy-done | bytes 2072
  0.7 0.0 copy-done.5
  0.7 0.0 copy-done.8
  0.7 0.0 copy-done.9
  0.7 0.0 copy-start
  0.7 0.9 %copy-done = f32[128,512]{1,0:T(8,128)S(1)} copy-done((f32[128,512]{1,0:T(8,128)S(1)}, f32[128,512]{1,0:T(8,128)}, u32[]{:S(2)}) %copy-start) | copy-done | bytes 262168
  1.7 0.0 copy-start.1
  1.7 0.9 %copy-done.1 = f32[4,128,128]{2,1,0:T(8,128)S(1)} copy-done((f32[4,128,128]{2,1,0:T(8,128)S(1)}, f32[4,128,128]{2,1,0:T(8,128)}, u32[]{:S(2)}) %copy-start.1) | copy-done | bytes 262168
  2.6 0.0 copy-start.2
  2.6 0.7 %copy-done.2 = f32[4096]{0:T(1024)S(1)} copy-done((f32[4096]{0:T(1024)S(1)}, f32[4096]{0:T(1024)}, u32[]{:S(2)}) %copy-start.2) | copy-done | bytes 16408
  3.3 0.0 copy-start.3
  3.3 0.7 %copy-done.3 = f32[4,512]{1,0:T(4,128)S(1)} copy-done((f32[4,512]{1,0:T(4,128)S(1)}, f32[4,512]{1,0:T(4,128)}, u32[]{:S(2)}) %copy-start.3) | copy-done | bytes 8216
  4.0 0.0 copy-start.4
  4.0 0.7 %copy-done.4 = f32[4,512]{1,0:T(4,128)S(1)} copy-done((f32[4,512]{1,0:T(4,128)S(1)}, f32[4,512]{1,0:T(4,128)}, u32[]{:S(2)}) %copy-start.4) | copy-done | bytes 8216
  4.7 0.0 copy-start.7
  4.7 0.7 %copy-done.7 = f32[512]{0:T(512)S(1)} copy-done((f32[512]{0:T(512)S(1)}, f32[512]{0:T(512)}, u32[]{:S(2)}) %copy-start.7) | copy-done | bytes 2072
  5.4 36.3 %sweep.1 = f32[128,512]{1,0:T(8,128)S(1)} custom-call(f32[128,512]{1,0:T(8,128)S(1)} %copy-done, bf16[4,8,128,128]{3,2,1,0:T(8,128)(2,1)} %coupling.1, s32[4,8]{1,0:T(4,128)S(1)} %copy-done.5, f32[1,512]{1,0:T(1,128)S(1)} %bitcast.4, f32[1,4096]{1,0:T(1,128)S(1)} %bitcast.3, s32[4]{0:T(128)S(1)} %copy-done.8, f32[1,512]{1,0:T(1,128)S(1)} %bitcast.5, ...), custom_call_target="tpu_custom_call" | custom-call | tf_op jit(solution)/shard_map/sweep/pallas_call | solution.py:487
  41.7 0.7 %copy.13 = f32[128,512]{1,0:T(8,128)} copy(f32[128,512]{1,0:T(8,128)S(1)} %sweep.1) | data formatting | bytes 524288
Async XLA Ops:
  0.0 0.7 %copy-start.6 = (f32[512]{0:T(512)S(1)}, f32[512]{0:T(512)}, u32[]{:S(2)}) copy-start(f32[512]{0:T(512)} %param.14) | copy-start | bytes 6148
  0.0 0.7 %copy-start.5 = (s32[4,8]{1,0:T(4,128)S(1)}, s32[4,8]{1,0:T(4,128)}, u32[]{:S(2)}) copy-start(s32[4,8]{1,0:T(4,128)} %pattern.1) | copy-start | bytes 388
  0.0 0.7 %copy-start.8 = (s32[4]{0:T(128)S(1)}, s32[4]{0:T(128)}, u32[]{:S(2)}) copy-start(s32[4]{0:T(128)} %direction.1) | copy-start | bytes 52
  0.0 0.7 %copy-start.9 = (s32[16]{0:T(128)S(1)}, s32[16]{0:T(128)}, u32[]{:S(2)}) copy-start(s32[16]{0:T(128)} %front.1) | copy-start | bytes 196
  0.7 1.0 %copy-start = (f32[128,512]{1,0:T(8,128)S(1)}, f32[128,512]{1,0:T(8,128)}, u32[]{:S(2)}) copy-start(f32[128,512]{1,0:T(8,128)} %occupation.1) | copy-start | bytes 786436
  1.7 0.9 %copy-start.1 = (f32[4,128,128]{2,1,0:T(8,128)S(1)}, f32[4,128,128]{2,1,0:T(8,128)}, u32[]{:S(2)}) copy-start(f32[4,128,128]{2,1,0:T(8,128)} %inscatter.1) | copy-start | bytes 786436
  2.6 0.7 %copy-start.2 = (f32[4096]{0:T(1024)S(1)}, f32[4096]{0:T(1024)}, u32[]{:S(2)}) copy-start(f32[4096]{0:T(1024)} %param.15) | copy-start | bytes 49156
  3.3 0.7 %copy-start.3 = (f32[4,512]{1,0:T(4,128)S(1)}, f32[4,512]{1,0:T(4,128)}, u32[]{:S(2)}) copy-start(f32[4,512]{1,0:T(4,128)} %inflow_low.1) | copy-start | bytes 24580
  4.0 0.7 %copy-start.4 = (f32[4,512]{1,0:T(4,128)S(1)}, f32[4,512]{1,0:T(4,128)}, u32[]{:S(2)}) copy-start(f32[4,512]{1,0:T(4,128)} %inflow_high.1) | copy-start | bytes 24580
  4.7 0.7 %copy-start.7 = (f32[512]{0:T(512)S(1)}, f32[512]{0:T(512)}, u32[]{:S(2)}) copy-start(f32[512]{0:T(512)} %param.17) | copy-start | bytes 6148

commit v3 on v2

--- a/solution.py
+++ b/solution.py
@@ -169,6 +169,8 @@
     from_mate,
     from_left,
     from_right,
+    direct_left,
+    direct_right,
     source,
     local,
     wall_part,
@@ -183,6 +185,8 @@
     line_send,
     left_recv,
     right_recv,
+    direct_send,
+    direct_recv,
     face_send,
     face_recv,
 ):
@@ -280,17 +284,76 @@
             device_id_type=MESH,
         )
 
+    def direct_copy(step):
+        return pltpu.make_async_remote_copy(
+            src_ref=part.at[mate + 2 * step, rows_of(1)],
+            dst_ref=direct_left if step > 0 else direct_right,
+            send_sem=direct_send.at[max(step, 0)],
+            recv_sem=direct_recv.at[max(step, 0)],
+            device_id={"modes": me + 2 * step},
+            device_id_type=MESH,
+        )
+
+    def arrival(buffer, sem):
+        return pltpu.make_async_remote_copy(
+            src_ref=buffer,
+            dst_ref=buffer,
+            send_sem=direct_send.at[0],
+            recv_sem=sem,
+            device_id={"modes": mate},
+            device_id_type=MESH,
+        )
+
+    def mate_items(at):
+        return [
+            (place, half)
+            for place in orders[at]
+            for half in range(2)
+            if half == 0 or abs(place - at) != 1
+        ]
+
+    def each_line(action):
+        for at in range(lines):
+            pl.when(z == at)(functools.partial(action, at))
+
+    def start_direct(at):
+        if at > 0:
+            direct_copy(-1).start()
+        if at < lines - 1:
+            direct_copy(1).start()
+
+    def start_mate(at, index):
+        items = mate_items(at)
+        if index < len(items):
+            place, half = items[index]
+            if (place, half) == (at, 1):
+                total = part[2 * at + 1 - y, rows_of(1)]
+                if at > 0:
+                    arrival(direct_left, direct_recv.at[1]).wait_recv()
+                    total = total + direct_left[...]
+                if at < lines - 1:
+                    arrival(direct_right, direct_recv.at[0]).wait_recv()
+                    total = total + direct_right[...]
+                part[2 * at + 1 - y, rows_of(1)] = total
+            mate_copy(place, half).start()
+
     make_part(destinations[0])
     pl.semaphore_wait(
         barrier, slabs + (z > 0).astype(jnp.int32) + (z < lines - 1).astype(jnp.int32)
     )
-    for half in range(2):
-        mate_copy(places[0], half).start()
+    if lines > 3:
+        for half in range(2):
+            mate_copy(places[0], half).start()
     for step in range(1, len(destinations)):
         make_part(destinations[step])
-        if step == 1:
-            for half in range(2):
-                mate_copy(places[1], half).start()
+        if step == lines - 1:
+            each_line(start_direct)
+
+            def start_early(at):
+                for index in range(2 if lines > 3 else 0, 4):
+                    start_mate(at, index)
+
+            each_line(start_early)
 
     row_id = lax.broadcasted_iota(jnp.int32, (BLK, BLK), 0)
     column_id = lax.broadcasted_iota(jnp.int32, (BLK, BLK), 1)
@@ -333,19 +396,19 @@
 
     def reduce_at(at, first, last):
         items = [(place, half) for place in orders[at] for half in range(2)]
-        for index, (place, half) in enumerate(items[:last]):
-            if index < first:
-                continue
-            mate_copy(place, half).wait_recv()
-            if index + 4 < len(items):
-                mate_copy(*items[index + 4]).start()
+        by_mate = mate_items(at)
+        for place, half in items[first:last]:
             rows = rows_of(half)
-            total = part[2 * place + y, rows] + from_mate[place, rows]
+            total = part[2 * place + y, rows]
+            if (place, half) in by_mate:
+                mate_copy(place, half).wait_recv()
+                start_mate(at, by_mate.index((place, half)) + 4)
+                total = total + from_mate[place, rows]
             if place >= at > 0:
-                line_copy(place, half, 1).wait_recv()
+                arrival(from_left.at[place, rows], left_recv.at[place, half]).wait_recv()
                 total = total + from_left[place, rows]
             if place <= at < lines - 1:
-                line_copy(place, half, -1).wait_recv()
+                arrival(from_right.at[place, rows], right_recv.at[place, half]).wait_recv()
                 total = total + from_right[place, rows]
             if place == at:
                 source[rows] = total
@@ -355,8 +418,7 @@
 
     edges = [0, 1, 2, 3, 4, 2 * lines]
     for step in range(len(edges) - 1):
-        for at in range(lines):
-            pl.when(z == at)(functools.partial(reduce_at, at, edges[step], edges[step + 1]))
+        each_line(functools.partial(reduce_at, first=edges[step], last=edges[step + 1]))
         if step < SHELL:
             prepare(step)
 
@@ -428,18 +490,19 @@
         swept = local[:, lanes(block)] + added
         out[:, lanes(block)] = jnp.where(upward(block), swept, turned(swept))
 
-    for place in range(lines):
-        for half in range(2):
+    def finish_at(at):
+        for place, half in mate_items(at):
             mate_copy(place, half).wait_send()
-
-    def finish_at(at):
+        if at > 0:
+            direct_copy(-1).wait_send()
+        if at < lines - 1:
+            direct_copy(1).wait_send()
         for place in range(lines):
             if place != at:
                 for half in range(2):
                     line_copy(place, half, 1 if place > at else -1).wait_send()
 
-    for at in range(lines):
-        pl.when(z == at)(functools.partial(finish_at, at))
+    each_line(finish_at)
     for away in range(1, slabs):
         face_copy(away).wait_send()
 
@@ -486,7 +549,7 @@
     dma = pltpu.SemaphoreType.DMA
     return pl.pallas_call(
         functools.partial(kernel, lines, slabs),
-        out_shape=jax.ShapeDtypeStruct((cells, width), f32),
+        out_shape=pltpu.VMEM((cells, width), f32),
         in_specs=[vmem, far, smem, vmem, vmem, smem, vmem, vmem, vmem, vmem, smem],
         out_specs=vmem,
         scratch_shapes=[
@@ -495,6 +558,8 @@
             pltpu.VMEM((lines, cells, width), f32),
             pltpu.VMEM((lines, cells, width), f32),
             pltpu.VMEM((lines, cells, width), f32),
+            pltpu.VMEM((cells // 2, width), f32),
+            pltpu.VMEM((cells // 2, width), f32),
             pltpu.VMEM((cells, width), f32),
             pltpu.VMEM((cells, width), f32),
             pltpu.VMEM((lateral, width), f32),
@@ -509,11 +574,13 @@
             dma((lines, 2)),
             dma((lines, 2)),
             dma((lines, 2)),
+            dma((2,)),
+            dma((2,)),
             dma((max(slabs - 1, 1),)),
             dma((slabs,)),
         ],
         compiler_params=pltpu.CompilerParams(
-            collective_id=0, has_side_effects=True, vmem_limit_bytes=53 * 2**20
+            collective_id=0, has_side_effects=True, vmem_limit_bytes=56 * 2**20
         ),
         name="sweep",
     )(

time: 42.8 us -> 37.8 us (0.88)
  local copies, waits for them, and re-layouts: 6.09 us -> 0.71 us
  Pallas kernels: 36.3 us -> 36.9 us
    unnamed x21 -> x1, local copies, waits for them, and re-layouts: 6.09 us -> 0.71 us
    pallas_call x1, Pallas kernels: 36.3 us -> 36.9 us  [per_device(): pl.pallas_call(functools.partial(kernel, lines, slabs), out_shape=pltpu.V...]
where the time goes in v3:
time: 37.8 us; the launch traced here: 37.6 us
  Pallas kernels  36.9 us (98%)
  local copies, waits for them, and re-layouts  0.71 us (2%)
    pallas_call x1, Pallas kernels, per_device(): pl.pallas_call(functools.partial(kernel, lines, slabs), out_shape=pltpu.V...  36.9 us

profile of v3, /device:TPU:0, one launch (start us, length us, event | category | flops | bytes accessed | tf_op | source)
XLA Modules:
  0.0 37.6 jit_solution(9186437811535874812)
XLA Ops:
  0.0 36.9 %sweep.1 = f32[128,512]{1,0:T(8,128)S(1)} custom-call(f32[128,512]{1,0:T(8,128)} %occupation.1, bf16[4,8,128,128]{3,2,1,0:T(8,128)(2,1)} %coupling.1, s32[4,8]{1,0:T(4,128)} %pattern.1, f32[1,512]{1,0:T(1,128)} %bitcast.4, f32[1,4096]{1,0:T(1,128)} %bitcast.3, s32[4]{0:T(128)} %direction.1, f32[1,512]{1,0:T(1,128)} %bitcast.5, f32[4,128,128]{2,1,0:T(8,128)} %inscatter.1, ...), custom_call_target="tpu_custom_call" | custom-call | tf_op jit(solution)/shard_map/sweep/pallas_call | solution.py:550
  36.9 0.7 %copy.13 = f32[128,512]{1,0:T(8,128)} copy(f32[128,512]{1,0:T(8,128)S(1)} %sweep.1) | data formatting | bytes 524288

commit v4 on v3

--- a/solution.py
+++ b/solution.py
@@ -144,9 +144,8 @@
 
 
 def visiting_order(z, count):
-    right = list(range(count - 1, z, -1))
-    left = list(range(z))
-    return (right + left if 2 * z < count else left + right) + [z]
+    side = 1 if 2 * z < count else -1
+    return sorted(range(count), key=lambda place: (-abs(place - z), side * place))
 
 
 def kernel(
@@ -172,6 +171,7 @@
     direct_left,
     direct_right,
     source,
+    climbed,
     local,
     wall_part,
     walls,
@@ -416,29 +416,66 @@
                 part[2 * place + y, rows] = total
                 line_copy(place, half, 1 if place > at else -1).start()
 
-    edges = [0, 1, 2, 3, 4, 2 * lines]
+    edges = [0, 1, 2, 3, 4, 2 * lines - 1]
     for step in range(len(edges) - 1):
         each_line(functools.partial(reduce_at, first=edges[step], last=edges[step + 1]))
         if step < SHELL:
             prepare(step)
 
+    def strips(values):
+        return [
+            values[at * lateral : (at + 1) * lateral] for at in range(values.shape[0] // lateral)
+        ]
+
+    def joined(parts):
+        return parts[0] if len(parts) == 1 else jnp.concatenate(parts, axis=0)
+
     def turned(values):
+        return joined(strips(values)[::-1])
+
+    blocks = range(SHELL)
+
+    def climb(half):
+        level = []
+        for block in blocks:
+            given = source[rows_of(half), lanes(block)]
+            level.append(jnp.where(upward(block), given, turned(given)))
+        level = [level[block] + product(level[block], scatter_table[block]) for block in blocks]
+        reach, base = 1, 0
+        while True:
+            size = level[0].shape[0]
+            for block in blocks:
+                climbed[half, base : base + size, lanes(block)] = level[block]
+            if size == lateral:
+                return
+            base += size
+            level = [
+                joined(strips(level[block])[1::2])
+                + product(joined(strips(level[block])[::2]), power_table[block, reach - 1])
+                for block in blocks
+            ]
+            reach *= 2
+
+    climb(0)
+    each_line(functools.partial(reduce_at, first=2 * lines - 1, last=2 * lines))
+    climb(1)
+
+    def tier(block, base, size):
+        one, two = (climbed[half, base : base + size, lanes(block)] for half in range(2))
         return jnp.concatenate(
-            [values[at * lateral : (at + 1) * lateral] for at in reversed(range(layers))], axis=0
-        )
-
-    for block in range(SHELL):
-        given = source[:, lanes(block)]
-        given = jnp.where(upward(block), given, turned(given))
-        swept = given + product(given, scatter_table[block])
-        reach = 1
-        while reach < layers:
-            edge = reach * lateral
-            moved = product(swept[: cells - edge], power_table[block, reach - 1])
-            swept = jnp.concatenate([swept[:edge], swept[edge:] + moved], axis=0)
-            reach *= 2
-        local[:, lanes(block)] = swept
-        faces[slab, :, lanes(block)] = swept[cells - lateral :]
+            [jnp.where(upward(block), one, two), jnp.where(upward(block), two, one)], axis=0
+        )
+
+    tiers, base, size = [], 0, piece
+    while size >= lateral:
+        tiers.append((base, size))
+        base, size = base + size, size // 2
+    prefix = []
+    for block in blocks:
+        low, high = strips(tier(block, *tiers[-1]))
+        face = high + product(low, power_table[block, layers // 2 - 1])
+        faces[slab, :, lanes(block)] = face
+        prefix.append([face])
 
     def face_copy(away):
         return pltpu.make_async_remote_copy(
@@ -452,6 +489,22 @@
 
     for away in range(1, slabs):
         face_copy(away).start()
+
+    reach = layers // 2
+    for base, size in reversed(tiers):
+        for block in blocks:
+            sums = strips(tier(block, base, size))
+            known = prefix[block]
+            line = [sums[0], known[0]]
+            if len(known) > 1:
+                moved = strips(product(joined(known[:-1]), power_table[block, reach - 1]))
+                for at in range(1, len(known)):
+                    line += [sums[2 * at] + moved[at - 1], known[at]]
+            prefix[block] = line
+        reach //= 2
+    for block in blocks:
+        local[:, lanes(block)] = joined(prefix[block])
+
     for away in range(1, slabs):
         sender = lax.rem(slab + away, slabs)
         pltpu.make_async_remote_copy(
@@ -463,8 +516,9 @@
             device_id_type=MESH,
         ).wait_recv()
 
-    for block in range(SHELL):
-        arrived = jnp.zeros((lateral, BLK), jnp.float32)
+    inflows = []
+    for block in blocks:
+        inflow = wall_part[:, lanes(block)]
         for away in range(slabs - 1):
             sender = rank(block) - 1 - away
             face = jnp.zeros((lateral, BLK), jnp.float32)
@@ -478,15 +532,10 @@
                     ),
                     face,
                 )
-            arrived += product(face, leap_table[block, away - 1]) if away else face
-        inflow = arrived + wall_part[:, lanes(block)]
-        added = jnp.concatenate(
-            [
-                product(inflow, power_table[block, at])
-                for at in range(layers)
-            ],
-            axis=0,
-        )
+            inflow += product(face, leap_table[block, away - 1]) if away else face
+        inflows.append(inflow)
+    for block in blocks:
+        added = joined([product(inflows[block], power_table[block, at]) for at in range(layers)])
         swept = local[:, lanes(block)] + added
         out[:, lanes(block)] = jnp.where(upward(block), swept, turned(swept))
 
@@ -528,7 +577,7 @@
     layers = cells // lateral
     block_bytes = 4 * cells * width
     needed = block_bytes * (groups + 3 * lines) + 2 * coupling.size
-    if groups % 2 or layers & (layers - 1) or needed > KERNEL_BUFFER_BYTES:
+    if groups % 2 or layers < 2 or layers & (layers - 1) or needed > KERNEL_BUFFER_BYTES:
         return per_device_plain(
             occupation_prior,
             coupling,
@@ -561,6 +610,7 @@
             pltpu.VMEM((cells // 2, width), f32),
             pltpu.VMEM((cells // 2, width), f32),
             pltpu.VMEM((cells, width), f32),
+            pltpu.VMEM((2, cells, width), f32),
             pltpu.VMEM((cells, width), f32),
             pltpu.VMEM((lateral, width), f32),
             pltpu.VMEM((2, lateral, width), f32),

time: 37.8 us -> 34.4 us (0.910)
  the two profiles are of different devices: /device:TPU:0 before, /device:TPU:21 now
where the time goes in v4:
time: 34.4 us; the launch traced here: 34.2 us
  Pallas kernels  33.5 us (97%)
  local copies, waits for them, and re-layouts  0.71 us (2%)
    pallas_call x1, Pallas kernels, per_device(): pl.pallas_call(functools.partial(kernel, lines, slabs), out_shape=pltpu.V...  33.5 us
    unnamed x1, local copies, waits for them, and re-layouts  0.71 us

profile of v4, /device:TPU:21, one launch (start us, length us, event | category | flops | bytes accessed | tf_op | source)
XLA Modules:
  0.0 34.2 jit_solution(789607585886668401)
XLA Ops:
  0.0 33.5 %sweep.1 = f32[128,512]{1,0:T(8,128)S(1)} custom-call(f32[128,512]{1,0:T(8,128)} %occupation.1, bf16[4,8,128,128]{3,2,1,0:T(8,128)(2,1)} %coupling.1, s32[4,8]{1,0:T(4,128)} %pattern.1, f32[1,512]{1,0:T(1,128)} %bitcast.4, f32[1,4096]{1,0:T(1,128)} %bitcast.3, s32[4]{0:T(128)} %direction.1, f32[1,512]{1,0:T(1,128)} %bitcast.5, f32[4,128,128]{2,1,0:T(8,128)} %inscatter.1, ...), custom_call_target="tpu_custom_call" | custom-call | tf_op jit(solution)/shard_map/sweep/pallas_call | solution.py:599
  33.5 0.7 %copy.13 = f32[128,512]{1,0:T(8,128)} copy(f32[128,512]{1,0:T(8,128)S(1)} %sweep.1) | data formatting | bytes 524288

commit v5 on v4

--- a/solution.py
+++ b/solution.py
@@ -125,22 +125,15 @@
 
 
 def packed(matrix):
-    high, low = halves(matrix)
-    return jnp.concatenate(
-        [
-            jnp.concatenate([high, low], axis=1),
-            jnp.concatenate([high, jnp.zeros_like(low)], axis=1),
-        ],
-        axis=0,
-    )
+    return jnp.concatenate(halves(matrix), axis=1)
 
 
 def product(left, right):
+    rows, width = left.shape[0], right.shape[1] // 2
     terms = jnp.dot(
-        jnp.concatenate(halves(left), axis=1), right, preferred_element_type=jnp.float32
-    )
-    width = terms.shape[1] // 2
-    return terms[:, :width] + terms[:, width:]
+        jnp.concatenate(halves(left), axis=0), right, preferred_element_type=jnp.float32
+    )
+    return terms[:rows, :width] + (terms[rows:, :width] + terms[:rows, width:])
 
 
 def visiting_order(z, count):
@@ -151,18 +144,11 @@
 def kernel(
     lines,
     slabs,
-    occupation,
+    operands,
     coupling,
-    pattern,
-    weights,
-    slope,
-    direction,
-    rate,
-    inscatter,
-    inflow_low,
-    inflow_high,
-    front,
     out,
+    copies,
+    copy_sem,
     held,
     part,
     from_mate,
@@ -190,10 +176,12 @@
     face_send,
     face_recv,
 ):
+    occupation, pattern, weights, slope, direction, rate, inscatter, inflow_low, inflow_high, front = copies
     cells, width = occupation.shape
     lateral = front.shape[0]
     layers = cells // lateral
     piece = cells // 2
+    detour = 3 * cells // 8
     me = lax.axis_index("modes")
     slab = lax.axis_index("slab")
     z, y = lax.div(me, 2), lax.rem(me, 2)
@@ -213,8 +201,18 @@
     def fetch(group):
         return pltpu.make_async_copy(coupling.at[:, group], held.at[group], coupling_sem.at[group])
 
-    for group in destinations:
+    loads = [
+        pltpu.make_async_copy(operands[at], copies[at], copy_sem.at[at])
+        for at in range(len(copies))
+    ]
+    first_loads = 4
+    fetch(destinations[0]).start()
+    for load in loads[:first_loads]:
+        load.start()
+    for group in destinations[1:]:
         fetch(group).start()
+    for load in loads[first_loads:]:
+        load.start()
 
     barrier = pltpu.get_barrier_semaphore()
     pl.semaphore_signal(barrier, inc=1, device_id={"modes": mate}, device_id_type=MESH)
@@ -235,6 +233,8 @@
             device_id_type=MESH,
         )
 
+    for load in loads[:first_loads]:
+        load.wait()
     prior = occupation[...]
     rounded = prior.astype(jnp.bfloat16)
     warmth = jnp.sum(prior * weights[...], axis=1, keepdims=True)
@@ -264,10 +264,11 @@
     def rows_of(half):
         return pl.ds(half * piece, piece)
 
-    def mate_copy(place, half):
+    def mate_copy(place, half, short=False):
+        rows = pl.ds(piece, piece - detour) if short else rows_of(half)
         return pltpu.make_async_remote_copy(
-            src_ref=part.at[2 * place + 1 - y, rows_of(half)],
-            dst_ref=from_mate.at[place, rows_of(half)],
+            src_ref=part.at[2 * place + 1 - y, rows],
+            dst_ref=from_mate.at[place, rows],
             send_sem=mate_send.at[place, half],
             recv_sem=mate_recv.at[place, half],
             device_id={"modes": mate},
@@ -286,7 +287,7 @@
 
     def direct_copy(step):
         return pltpu.make_async_remote_copy(
-            src_ref=part.at[mate + 2 * step, rows_of(1)],
+            src_ref=part.at[mate + 2 * step, pl.ds(cells - detour, detour)],
             dst_ref=direct_left if step > 0 else direct_right,
             send_sem=direct_send.at[max(step, 0)],
             recv_sem=direct_recv.at[max(step, 0)],
@@ -306,10 +307,9 @@
 
     def mate_items(at):
         return [
-            (place, half)
+            (place, half, half == 1 and abs(place - at) == 1)
             for place in orders[at]
             for half in range(2)
-            if half == 0 or abs(place - at) != 1
         ]
 
     def each_line(action):
@@ -325,17 +325,18 @@
     def start_mate(at, index):
         items = mate_items(at)
         if index < len(items):
-            place, half = items[index]
+            place, half, short = items[index]
             if (place, half) == (at, 1):
-                total = part[2 * at + 1 - y, rows_of(1)]
+                rows = pl.ds(cells - detour, detour)
+                total = part[2 * at + 1 - y, rows]
                 if at > 0:
                     arrival(direct_left, direct_recv.at[1]).wait_recv()
                     total = total + direct_left[...]
                 if at < lines - 1:
                     arrival(direct_right, direct_recv.at[0]).wait_recv()
                     total = total + direct_right[...]
-                part[2 * at + 1 - y, rows_of(1)] = total
-            mate_copy(place, half).start()
+                part[2 * at + 1 - y, rows] = total
+            mate_copy(place, half, short).start()
 
     make_part(destinations[0])
     pl.semaphore_wait(
@@ -355,6 +356,8 @@
 
             each_line(start_early)
 
+    for load in loads[first_loads:]:
+        load.wait()
     row_id = lax.broadcasted_iota(jnp.int32, (BLK, BLK), 0)
     column_id = lax.broadcasted_iota(jnp.int32, (BLK, BLK), 1)
     for row in range(lateral):
@@ -395,15 +398,16 @@
         wall_part[:, lanes(block)] = carried
 
     def reduce_at(at, first, last):
-        items = [(place, half) for place in orders[at] for half in range(2)]
-        by_mate = mate_items(at)
-        for place, half in items[first:last]:
+        for index, (place, half, short) in list(enumerate(mate_items(at)))[first:last]:
             rows = rows_of(half)
-            total = part[2 * place + y, rows]
-            if (place, half) in by_mate:
-                mate_copy(place, half).wait_recv()
-                start_mate(at, by_mate.index((place, half)) + 4)
-                total = total + from_mate[place, rows]
+            mate_copy(place, half, short).wait_recv()
+            start_mate(at, index + 4)
+            if short:
+                straight = pl.ds(piece, piece - detour)
+                part[2 * place + y, straight] += from_mate[place, straight]
+                total = part[2 * place + y, rows]
+            else:
+                total = part[2 * place + y, rows] + from_mate[place, rows]
             if place >= at > 0:
                 arrival(from_left.at[place, rows], left_recv.at[place, half]).wait_recv()
                 total = total + from_left[place, rows]
@@ -540,8 +544,8 @@
         out[:, lanes(block)] = jnp.where(upward(block), swept, turned(swept))
 
     def finish_at(at):
-        for place, half in mate_items(at):
-            mate_copy(place, half).wait_send()
+        for item in mate_items(at):
+            mate_copy(*item).wait_send()
         if at > 0:
             direct_copy(-1).wait_send()
         if at < lines - 1:
@@ -577,7 +581,7 @@
     layers = cells // lateral
     block_bytes = 4 * cells * width
     needed = block_bytes * (groups + 3 * lines) + 2 * coupling.size
-    if groups % 2 or layers < 2 or layers & (layers - 1) or needed > KERNEL_BUFFER_BYTES:
+    if groups % 2 or layers < 2 or layers & (layers - 1) or cells % 64 or needed > KERNEL_BUFFER_BYTES:
         return per_device_plain(
             occupation_prior,
             coupling,
@@ -592,32 +596,48 @@
             front_of_row,
         )
     vmem = pl.BlockSpec(memory_space=pltpu.VMEM)
-    smem = pl.BlockSpec(memory_space=pltpu.SMEM)
     far = pl.BlockSpec(memory_space=pl.ANY)
-    f32, bf16 = jnp.float32, jnp.bfloat16
+    f32, bf16, i32 = jnp.float32, jnp.bfloat16, jnp.int32
+    operands = (
+        occupation_prior,
+        pattern,
+        pseudo_weights.reshape(1, width),
+        equilibrium_slope.reshape(1, groups * width),
+        direction,
+        stream_rate.reshape(1, width),
+        inscatter,
+        inflow_low,
+        inflow_high,
+        front_of_row,
+    )
     dma = pltpu.SemaphoreType.DMA
     return pl.pallas_call(
         functools.partial(kernel, lines, slabs),
         out_shape=pltpu.VMEM((cells, width), f32),
-        in_specs=[vmem, far, smem, vmem, vmem, smem, vmem, vmem, vmem, vmem, smem],
+        in_specs=[(far,) * len(operands), far],
         out_specs=vmem,
         scratch_shapes=[
+            tuple(
+                (pltpu.SMEM if operand.dtype == i32 else pltpu.VMEM)(operand.shape, operand.dtype)
+                for operand in operands
+            ),
+            dma((len(operands),)),
             pltpu.VMEM((groups, SHELL, BLK, BLK), bf16),
             pltpu.VMEM((groups, cells, width), f32),
             pltpu.VMEM((lines, cells, width), f32),
             pltpu.VMEM((lines, cells, width), f32),
             pltpu.VMEM((lines, cells, width), f32),
-            pltpu.VMEM((cells // 2, width), f32),
-            pltpu.VMEM((cells // 2, width), f32),
+            pltpu.VMEM((3 * cells // 8, width), f32),
+            pltpu.VMEM((3 * cells // 8, width), f32),
             pltpu.VMEM((cells, width), f32),
             pltpu.VMEM((2, cells, width), f32),
             pltpu.VMEM((cells, width), f32),
             pltpu.VMEM((lateral, width), f32),
             pltpu.VMEM((2, lateral, width), f32),
             pltpu.VMEM((slabs, lateral, width), f32),
-            pltpu.VMEM((SHELL, 2 * BLK, 2 * BLK), bf16),
-            pltpu.VMEM((SHELL, layers, 2 * BLK, 2 * BLK), bf16),
-            pltpu.VMEM((SHELL, max(slabs - 2, 1), 2 * BLK, 2 * BLK), bf16),
+            pltpu.VMEM((SHELL, BLK, 2 * BLK), bf16),
+            pltpu.VMEM((SHELL, layers, BLK, 2 * BLK), bf16),
+            pltpu.VMEM((SHELL, max(slabs - 2, 1), BLK, 2 * BLK), bf16),
             dma((groups,)),
             dma((lines, 2)),
             dma((lines, 2)),
@@ -633,19 +653,7 @@
             collective_id=0, has_side_effects=True, vmem_limit_bytes=56 * 2**20
         ),
         name="sweep",
-    )(
-        occupation_prior,
-        coupling,
-        pattern,
-        pseudo_weights.reshape(1, width),
-        equilibrium_slope.reshape(1, groups * width),
-        direction,
-        stream_rate.reshape(1, width),
-        inscatter,
-        inflow_low,
-        inflow_high,
-        front_of_row,
-    )
+    )(operands, coupling)
 
 
 def solution(mesh):

time: 34.4 us -> 33.2 us (0.965)
  the two profiles are of different devices: /device:TPU:21 before, /device:TPU:17 now
where the time goes in v5:
time: 33.2 us; the launch traced here: 33.1 us
  Pallas kernels  32.4 us (98%)
  local copies, waits for them, and re-layouts  0.71 us (2%)
    pallas_call x1, Pallas kernels, per_device(): pl.pallas_call(functools.partial(kernel, lines, slabs), out_shape=pltpu.V...  32.4 us
    unnamed x1, local copies, waits for them, and re-layouts  0.71 us

profile of v5, /device:TPU:17, one launch (start us, length us, event | category | flops | bytes accessed | tf_op | source)
XLA Modules:
  0.0 33.1 jit_solution(251077524923249800)
XLA Ops:
  0.0 32.4 %sweep.1 = f32[128,512]{1,0:T(8,128)S(1)} custom-call(f32[128,512]{1,0:T(8,128)} %operands_0_.1, s32[4,8]{1,0:T(4,128)} %operands_1_.1, f32[1,512]{1,0:T(1,128)} %bitcast.4, f32[1,4096]{1,0:T(1,128)} %bitcast.3, s32[4]{0:T(128)} %operands_4_.1, f32[1,512]{1,0:T(1,128)} %bitcast.5, f32[4,128,128]{2,1,0:T(8,128)} %operands_6_.1, f32[4,512]{1,0:T(4,128)} %operands_7_.1, ...), custom_call_target="tpu_custom_call" | custom-call | tf_op jit(solution)/shard_map/sweep/pallas_call | solution.py:614
  32.4 0.7 %copy.13 = f32[128,512]{1,0:T(8,128)} copy(f32[128,512]{1,0:T(8,128)S(1)} %sweep.1) | data formatting | bytes 524288

commit v6 on v5

--- a/solution.py
+++ b/solution.py
@@ -181,11 +181,30 @@
     lateral = front.shape[0]
     layers = cells // lateral
     piece = cells // 2
-    detour = 3 * cells // 8
+    detour = cells // 4
     me = lax.axis_index("modes")
     slab = lax.axis_index("slab")
     z, y = lax.div(me, 2), lax.rem(me, 2)
     mate = 2 * z + 1 - y
+
+    barrier = pltpu.get_barrier_semaphore()
+    pl.semaphore_signal(barrier, inc=1, device_id={"modes": mate}, device_id_type=MESH)
+
+    @pl.when(z > 0)
+    def _():
+        pl.semaphore_signal(barrier, inc=1, device_id={"modes": me - 2}, device_id_type=MESH)
+
+    @pl.when(z < lines - 1)
+    def _():
+        pl.semaphore_signal(barrier, inc=1, device_id={"modes": me + 2}, device_id_type=MESH)
+
+    for away in range(1, slabs):
+        pl.semaphore_signal(
+            barrier,
+            inc=1,
+            device_id={"slab": lax.rem(slab + away, slabs)},
+            device_id_type=MESH,
+        )
 
     orders = [visiting_order(at, lines) for at in range(lines)]
 
@@ -196,7 +215,8 @@
         return spot
 
     places = [in_order(step) for step in range(lines)]
-    destinations = [2 * place + 1 - y for place in places] + [2 * place + y for place in places]
+    early = [places[0], *places[1:-1][::-1], places[-1]]
+    destinations = [2 * place + 1 - y for place in early] + [2 * place + y for place in places]
 
     def fetch(group):
         return pltpu.make_async_copy(coupling.at[:, group], held.at[group], coupling_sem.at[group])
@@ -213,25 +233,6 @@
         fetch(group).start()
     for load in loads[first_loads:]:
         load.start()
-
-    barrier = pltpu.get_barrier_semaphore()
-    pl.semaphore_signal(barrier, inc=1, device_id={"modes": mate}, device_id_type=MESH)
-
-    @pl.when(z > 0)
-    def _():
-        pl.semaphore_signal(barrier, inc=1, device_id={"modes": me - 2}, device_id_type=MESH)
-
-    @pl.when(z < lines - 1)
-    def _():
-        pl.semaphore_signal(barrier, inc=1, device_id={"modes": me + 2}, device_id_type=MESH)
-
-    for away in range(1, slabs):
-        pl.semaphore_signal(
-            barrier,
-            inc=1,
-            device_id={"slab": lax.rem(slab + away, slabs)},
-            device_id_type=MESH,
-        )
 
     for load in loads[:first_loads]:
         load.wait()
@@ -316,11 +317,9 @@
         for at in range(lines):
             pl.when(z == at)(functools.partial(action, at))
 
-    def start_direct(at):
-        if at > 0:
-            direct_copy(-1).start()
-        if at < lines - 1:
-            direct_copy(1).start()
+    def start_direct(at, nearest):
+        if nearest <= lines - 1 and abs(orders[at][-1 - nearest] - at) == 1:
+            direct_copy(orders[at][-1 - nearest] - at).start()
 
     def start_mate(at, index):
         items = mate_items(at)
@@ -342,16 +341,16 @@
     pl.semaphore_wait(
         barrier, slabs + (z > 0).astype(jnp.int32) + (z < lines - 1).astype(jnp.int32)
     )
-    if lines > 3:
-        for half in range(2):
-            mate_copy(places[0], half).start()
+    for half in range(2):
+        mate_copy(places[0], half).start()
     for step in range(1, len(destinations)):
         make_part(destinations[step])
+        if step <= 2:
+            each_line(functools.partial(start_direct, nearest=step))
         if step == lines - 1:
-            each_line(start_direct)
 
             def start_early(at):
-                for index in range(2 if lines > 3 else 0, 4):
+                for index in range(2, 4):
                     start_mate(at, index)
 
             each_line(start_early)
@@ -581,7 +580,7 @@
     layers = cells // lateral
     block_bytes = 4 * cells * width
     needed = block_bytes * (groups + 3 * lines) + 2 * coupling.size
-    if groups % 2 or layers < 2 or layers & (layers - 1) or cells % 64 or needed > KERNEL_BUFFER_BYTES:
+    if groups % 2 or lines < 4 or layers < 2 or layers & (layers - 1) or cells % 32 or needed > KERNEL_BUFFER_BYTES:
         return per_device_plain(
             occupation_prior,
             coupling,
@@ -627,8 +626,8 @@
             pltpu.VMEM((lines, cells, width), f32),
             pltpu.VMEM((lines, cells, width), f32),
             pltpu.VMEM((lines, cells, width), f32),
-            pltpu.VMEM((3 * cells // 8, width), f32),
-            pltpu.VMEM((3 * cells // 8, width), f32),
+            pltpu.VMEM((cells // 4, width), f32),
+            pltpu.VMEM((cells // 4, width), f32),
             pltpu.VMEM((cells, width), f32),
             pltpu.VMEM((2, cells, width), f32),
             pltpu.VMEM((cells, width), f32),

time: 33.2 us -> 33.2 us (level)
  no operation moved by 1% of the time
where the time goes in v6:
time: 33.2 us; the launch traced here: 33.1 us
  Pallas kernels  32.4 us (98%)
  local copies, waits for them, and re-layouts  0.71 us (2%)
    pallas_call x1, Pallas kernels, per_device(): pl.pallas_call(functools.partial(kernel, lines, slabs), out_shape=pltpu.V...  32.4 us
    unnamed x1, local copies, waits for them, and re-layouts  0.71 us

profile of v6, /device:TPU:17, one launch (start us, length us, event | category | flops | bytes accessed | tf_op | source)
XLA Modules:
  0.0 33.1 jit_solution(14369932838100787126)
XLA Ops:
  0.0 32.4 %sweep.1 = f32[128,512]{1,0:T(8,128)S(1)} custom-call(f32[128,512]{1,0:T(8,128)} %operands_0_.1, s32[4,8]{1,0:T(4,128)} %operands_1_.1, f32[1,512]{1,0:T(1,128)} %bitcast.4, f32[1,4096]{1,0:T(1,128)} %bitcast.3, s32[4]{0:T(128)} %operands_4_.1, f32[1,512]{1,0:T(1,128)} %bitcast.5, f32[4,128,128]{2,1,0:T(8,128)} %operands_6_.1, f32[4,512]{1,0:T(4,128)} %operands_7_.1, ...), custom_call_target="tpu_custom_call" | custom-call | tf_op jit(solution)/shard_map/sweep/pallas_call | solution.py:613
  32.4 0.7 %copy.13 = f32[128,512]{1,0:T(8,128)} copy(f32[128,512]{1,0:T(8,128)S(1)} %sweep.1) | data formatting | bytes 524288

commit v7 on v6

--- a/solution.py
+++ b/solution.py
@@ -181,7 +181,8 @@
     lateral = front.shape[0]
     layers = cells // lateral
     piece = cells // 2
-    detour = cells // 4
+    slips = range(4)
+    slip = detour = cells // len(slips)
     me = lax.axis_index("modes")
     slab = lax.axis_index("slab")
     z, y = lax.div(me, 2), lax.rem(me, 2)
@@ -265,8 +266,11 @@
     def rows_of(half):
         return pl.ds(half * piece, piece)
 
-    def mate_copy(place, half, short=False):
-        rows = pl.ds(piece, piece - detour) if short else rows_of(half)
+    def slip_rows(at):
+        return pl.ds(at * slip, slip)
+
+    def mate_copy(place, half):
+        rows = slip_rows(half)
         return pltpu.make_async_remote_copy(
             src_ref=part.at[2 * place + 1 - y, rows],
             dst_ref=from_mate.at[place, rows],
@@ -278,8 +282,8 @@
 
     def line_copy(place, half, step):
         return pltpu.make_async_remote_copy(
-            src_ref=part.at[2 * place + y, rows_of(half)],
-            dst_ref=(from_left if step > 0 else from_right).at[place, rows_of(half)],
+            src_ref=part.at[2 * place + y, slip_rows(half)],
+            dst_ref=(from_left if step > 0 else from_right).at[place, slip_rows(half)],
             send_sem=line_send.at[place, half],
             recv_sem=(left_recv if step > 0 else right_recv).at[place, half],
             device_id={"modes": me + 2 * step},
@@ -308,9 +312,10 @@
 
     def mate_items(at):
         return [
-            (place, half, half == 1 and abs(place - at) == 1)
+            (place, half)
             for place in orders[at]
-            for half in range(2)
+            for half in slips
+            if half < slips[-1] or abs(place - at) != 1
         ]
 
     def each_line(action):
@@ -324,8 +329,8 @@
     def start_mate(at, index):
         items = mate_items(at)
         if index < len(items):
-            place, half, short = items[index]
-            if (place, half) == (at, 1):
+            place, half = items[index]
+            if (place, half) == (at, slips[-1]):
                 rows = pl.ds(cells - detour, detour)
                 total = part[2 * at + 1 - y, rows]
                 if at > 0:
@@ -335,13 +340,13 @@
                     arrival(direct_right, direct_recv.at[0]).wait_recv()
                     total = total + direct_right[...]
                 part[2 * at + 1 - y, rows] = total
-            mate_copy(place, half, short).start()
+            mate_copy(place, half).start()
 
     make_part(destinations[0])
     pl.semaphore_wait(
         barrier, slabs + (z > 0).astype(jnp.int32) + (z < lines - 1).astype(jnp.int32)
     )
-    for half in range(2):
+    for half in slips:
         mate_copy(places[0], half).start()
     for step in range(1, len(destinations)):
         make_part(destinations[step])
@@ -350,7 +355,7 @@
         if step == lines - 1:
 
             def start_early(at):
-                for index in range(2, 4):
+                for index in range(len(slips), 2 * len(slips)):
                     start_mate(at, index)
 
             each_line(start_early)
@@ -397,16 +402,15 @@
         wall_part[:, lanes(block)] = carried
 
     def reduce_at(at, first, last):
-        for index, (place, half, short) in list(enumerate(mate_items(at)))[first:last]:
-            rows = rows_of(half)
-            mate_copy(place, half, short).wait_recv()
-            start_mate(at, index + 4)
-            if short:
-                straight = pl.ds(piece, piece - detour)
-                part[2 * place + y, straight] += from_mate[place, straight]
-                total = part[2 * place + y, rows]
-            else:
-                total = part[2 * place + y, rows] + from_mate[place, rows]
+        items = [(place, half) for place in orders[at] for half in slips]
+        by_mate = mate_items(at)
+        for place, half in items[first:last]:
+            rows = slip_rows(half)
+            total = part[2 * place + y, rows]
+            if (place, half) in by_mate:
+                mate_copy(place, half).wait_recv()
+                start_mate(at, by_mate.index((place, half)) + 2 * len(slips))
+                total = total + from_mate[place, rows]
             if place >= at > 0:
                 arrival(from_left.at[place, rows], left_recv.at[place, half]).wait_recv()
                 total = total + from_left[place, rows]
@@ -419,7 +423,7 @@
                 part[2 * place + y, rows] = total
                 line_copy(place, half, 1 if place > at else -1).start()
 
-    edges = [0, 1, 2, 3, 4, 2 * lines - 1]
+    edges = [0, 2, 4, 6, 8, 4 * lines - 2]
     for step in range(len(edges) - 1):
         each_line(functools.partial(reduce_at, first=edges[step], last=edges[step + 1]))
         if step < SHELL:
@@ -460,7 +464,7 @@
             reach *= 2
 
     climb(0)
-    each_line(functools.partial(reduce_at, first=2 * lines - 1, last=2 * lines))
+    each_line(functools.partial(reduce_at, first=4 * lines - 2, last=4 * lines))
     climb(1)
 
     def tier(block, base, size):
@@ -551,7 +555,7 @@
             direct_copy(1).wait_send()
         for place in range(lines):
             if place != at:
-                for half in range(2):
+                for half in slips:
                     line_copy(place, half, 1 if place > at else -1).wait_send()
 
     each_line(finish_at)
@@ -638,11 +642,11 @@
             pltpu.VMEM((SHELL, layers, BLK, 2 * BLK), bf16),
             pltpu.VMEM((SHELL, max(slabs - 2, 1), BLK, 2 * BLK), bf16),
             dma((groups,)),
-            dma((lines, 2)),
-            dma((lines, 2)),
-            dma((lines, 2)),
-            dma((lines, 2)),
-            dma((lines, 2)),
+            dma((lines, 4)),
+            dma((lines, 4)),
+            dma((lines, 4)),
+            dma((lines, 4)),
+            dma((lines, 4)),
             dma((2,)),
             dma((2,)),
             dma((max(slabs - 1, 1),)),

time: 33.2 us -> 32.5 us (0.979)
  the two profiles are of different devices: /device:TPU:17 before, /device:TPU:0 now
where the time goes in v7:
time: 32.5 us; the launch traced here: 32.4 us
  Pallas kernels  31.7 us (98%)
  local copies, waits for them, and re-layouts  0.71 us (2%)
    pallas_call x1, Pallas kernels, per_device(): pl.pallas_call(functools.partial(kernel, lines, slabs), out_shape=pltpu.V...  31.7 us
    unnamed x1, local copies, waits for them, and re-layouts  0.71 us

profile of v7, /device:TPU:0, one launch (start us, length us, event | category | flops | bytes accessed | tf_op | source)
XLA Modules:
  0.0 32.4 jit_solution(4110206302530258572)
XLA Ops:
  0.0 31.7 %sweep.1 = f32[128,512]{1,0:T(8,128)S(1)} custom-call(f32[128,512]{1,0:T(8,128)} %operands_0_.1, s32[4,8]{1,0:T(4,128)} %operands_1_.1, f32[1,512]{1,0:T(1,128)} %bitcast.4, f32[1,4096]{1,0:T(1,128)} %bitcast.3, s32[4]{0:T(128)} %operands_4_.1, f32[1,512]{1,0:T(1,128)} %bitcast.5, f32[4,128,128]{2,1,0:T(8,128)} %operands_6_.1, f32[4,512]{1,0:T(4,128)} %operands_7_.1, ...), custom_call_target="tpu_custom_call" | custom-call | tf_op jit(solution)/shard_map/sweep/pallas_call | solution.py:617
  31.7 0.7 %copy.13 = f32[128,512]{1,0:T(8,128)} copy(f32[128,512]{1,0:T(8,128)S(1)} %sweep.1) | data formatting | bytes 524288

commit v8 on v7

--- a/solution.py
+++ b/solution.py
@@ -181,8 +181,9 @@
     lateral = front.shape[0]
     layers = cells // lateral
     piece = cells // 2
-    slips = range(4)
-    slip = detour = cells // len(slips)
+    slips = range(8)
+    slip = cells // len(slips)
+    detour = 3 * slip
     me = lax.axis_index("modes")
     slab = lax.axis_index("slab")
     z, y = lax.div(me, 2), lax.rem(me, 2)
@@ -315,7 +316,7 @@
             (place, half)
             for place in orders[at]
             for half in slips
-            if half < slips[-1] or abs(place - at) != 1
+            if half < slips[-3] or abs(place - at) != 1
         ]
 
     def each_line(action):
@@ -330,7 +331,7 @@
         items = mate_items(at)
         if index < len(items):
             place, half = items[index]
-            if (place, half) == (at, slips[-1]):
+            if (place, half) == (at, slips[-3]):
                 rows = pl.ds(cells - detour, detour)
                 total = part[2 * at + 1 - y, rows]
                 if at > 0:
@@ -423,7 +424,7 @@
                 part[2 * place + y, rows] = total
                 line_copy(place, half, 1 if place > at else -1).start()
 
-    edges = [0, 2, 4, 6, 8, 4 * lines - 2]
+    edges = [0, 4, 8, 12, 16, 8 * lines - 4]
     for step in range(len(edges) - 1):
         each_line(functools.partial(reduce_at, first=edges[step], last=edges[step + 1]))
         if step < SHELL:
@@ -464,7 +465,7 @@
             reach *= 2
 
     climb(0)
-    each_line(functools.partial(reduce_at, first=4 * lines - 2, last=4 * lines))
+    each_line(functools.partial(reduce_at, first=8 * lines - 4, last=8 * lines))
     climb(1)
 
     def tier(block, base, size):
@@ -584,7 +585,7 @@
     layers = cells // lateral
     block_bytes = 4 * cells * width
     needed = block_bytes * (groups + 3 * lines) + 2 * coupling.size
-    if groups % 2 or lines < 4 or layers < 2 or layers & (layers - 1) or cells % 32 or needed > KERNEL_BUFFER_BYTES:
+    if groups % 2 or lines < 4 or layers < 2 or layers & (layers - 1) or cells % 64 or needed > KERNEL_BUFFER_BYTES:
         return per_device_plain(
             occupation_prior,
             coupling,
@@ -630,8 +631,8 @@
             pltpu.VMEM((lines, cells, width), f32),
             pltpu.VMEM((lines, cells, width), f32),
             pltpu.VMEM((lines, cells, width), f32),
-            pltpu.VMEM((cells // 4, width), f32),
-            pltpu.VMEM((cells // 4, width), f32),
+            pltpu.VMEM((3 * cells // 8, width), f32),
+            pltpu.VMEM((3 * cells // 8, width), f32),
             pltpu.VMEM((cells, width), f32),
             pltpu.VMEM((2, cells, width), f32),
             pltpu.VMEM((cells, width), f32),
@@ -642,11 +643,11 @@
             pltpu.VMEM((SHELL, layers, BLK, 2 * BLK), bf16),
             pltpu.VMEM((SHELL, max(slabs - 2, 1), BLK, 2 * BLK), bf16),
             dma((groups,)),
-            dma((lines, 4)),
-            dma((lines, 4)),
-            dma((lines, 4)),
-            dma((lines, 4)),
-            dma((lines, 4)),
+            dma((lines, 8)),
+            dma((lines, 8)),
+            dma((lines, 8)),
+            dma((lines, 8)),
+            dma((lines, 8)),
             dma((2,)),
             dma((2,)),
             dma((max(slabs - 1, 1),)),

time: 32.5 us -> 32.6 us (level)
  no operation moved by 1% of the time
where the time goes in v8:
time: 32.6 us; the launch traced here: 32.5 us
  Pallas kernels  31.8 us (98%)
  local copies, waits for them, and re-layouts  0.71 us (2%)
    pallas_call x1, Pallas kernels, per_device(): pl.pallas_call(functools.partial(kernel, lines, slabs), out_shape=pltpu.V...  31.8 us
    unnamed x1, local copies, waits for them, and re-layouts  0.71 us

profile of v8, /device:TPU:0, one launch (start us, length us, event | category | flops | bytes accessed | tf_op | source)
XLA Modules:
  0.0 32.5 jit_solution(16364007665758328197)
XLA Ops:
  0.0 31.8 %sweep.1 = f32[128,512]{1,0:T(8,128)S(1)} custom-call(f32[128,512]{1,0:T(8,128)} %operands_0_.1, s32[4,8]{1,0:T(4,128)} %operands_1_.1, f32[1,512]{1,0:T(1,128)} %bitcast.4, f32[1,4096]{1,0:T(1,128)} %bitcast.3, s32[4]{0:T(128)} %operands_4_.1, f32[1,512]{1,0:T(1,128)} %bitcast.5, f32[4,128,128]{2,1,0:T(8,128)} %operands_6_.1, f32[4,512]{1,0:T(4,128)} %operands_7_.1, ...), custom_call_target="tpu_custom_call" | custom-call | tf_op jit(solution)/shard_map/sweep/pallas_call | solution.py:618
  31.8 0.7 %copy.13 = f32[128,512]{1,0:T(8,128)} copy(f32[128,512]{1,0:T(8,128)S(1)} %sweep.1) | data formatting | bytes 524288
